TPU v7x, 128 devices: a whole 4x4x4 slice. The times are simulated.
128 devices in a mesh: row: 8 (over y_lo, x), col: 16 (over z, y_hi, core).
Axes of the slice: x: 4, y: 4 (y_hi: 2, y_lo: 2; y = y_hi * 2 + y_lo), z: 4, core: 2. Of those that a mesh axis runs over, the one named last changes fastest.
Arguments:
- latents: bfloat16 [2, 512, 1024, 128], P(None, 'row', 'col'), may hold values from -6 to 6
- timesteps: int32 [2], replicated, may hold values from 0 to 999
- time_table: float32 [1000, 128], replicated, may hold values from -6 to 6
- conv_fine: bfloat16 [3, 3, 128, 128], replicated, may hold values from -0.1875 to 0.1875
- conv_coarse: bfloat16 [3, 3, 128, 256], replicated, may hold values from -0.1875 to 0.1875
- lift: float32 [256, 128], replicated, may hold values from -0.375 to 0.375
- cotangent: bfloat16 [2, 512, 1024, 128], P(None, 'row', 'col'), may hold values from -6 to 6
Outputs:
- latent_grad: float32 [2, 512, 1024, 128], P(None, 'row', 'col')
- fine_kernel_grad: float32 [3, 3, 128, 128], replicated
- coarse_kernel_grad: float32 [3, 3, 128, 256], replicated
- lift_grad: float32 [256, 128], replicated
- table_grad: float32 [1000, 128], replicated
All inputs are finite; a program needn't handle non-finite values.
Results may differ from a plain program's by a relative error of at most 0.014.
Values may be sent and summed in bfloat16 or wider, within the bound.
A program may use at most 128 MiB of HBM per device.

v0:
```python
import math

import jax
import jax.numpy as jnp
from jax import lax
from jax.sharding import PartitionSpec as P


def extended(x, sides, width):
    for axis, dim in sides:
        peers, length = (lax.axis_size(axis), x.shape[dim])
        up = [(i, (i + 1) % peers) for i in range(peers - 1)]
        down = [(j, i) for i, j in up]
        last = lax.slice_in_dim(x, length - width, length, axis=dim)
        first = lax.slice_in_dim(x, 0, width, axis=dim)
        before = lax.ppermute(last, axis, up)
        after = lax.ppermute(first, axis, down)
        x = jnp.concatenate([before, x, after], axis=dim)
    return x


def silu_slope(values):
    logistic = jax.nn.sigmoid(values)
    return logistic * (1.0 + values * (1.0 - logistic))


def forward_taps(padded, kernel, tile_rows, tile_cols):
    running = jnp.zeros(padded.shape[:1] + (tile_rows, tile_cols, kernel.shape[3]), jnp.float32)
    for row_tap in range(3):
        for col_tap in range(3):
            window = padded[:, row_tap : row_tap + tile_rows, col_tap : col_tap + tile_cols]
            running = running + jnp.einsum(
                "bhwc,cd->bhwd",
                window,
                kernel[row_tap, col_tap],
                preferred_element_type=jnp.float32,
            )
    return running


def back_taps(padded, kernel, tile_rows, tile_cols):
    running = jnp.zeros(padded.shape[:1] + (tile_rows, tile_cols, kernel.shape[2]), jnp.float32)
    for row_tap in range(3):
        for col_tap in range(3):
            window = padded[:, row_tap : row_tap + tile_rows, col_tap : col_tap + tile_cols]
            running = running + jnp.einsum(
                "bhwd,cd->bhwc",
                window,
                kernel[2 - row_tap, 2 - col_tap],
                preferred_element_type=jnp.float32,
            )
    return running


def weight_taps(padded, grad_in, tile_rows, tile_cols):
    pieces = []
    for row_tap in range(3):
        for col_tap in range(3):
            window = padded[:, row_tap : row_tap + tile_rows, col_tap : col_tap + tile_cols]
            pieces.append(
                jnp.einsum("bhwc,bhwd->cd", window, grad_in, preferred_element_type=jnp.float32)
            )
    return jnp.stack(pieces).reshape(3, 3, padded.shape[3], grad_in.shape[3])


def block_sum(field_in):
    count, tall, broad, chans = field_in.shape
    return (
        field_in.astype(jnp.float32)
        .reshape(count, tall // 2, 2, broad // 2, 2, chans)
        .sum(axis=(2, 4))
    )


def upsample(field_in):
    return jnp.repeat(jnp.repeat(field_in, 2, axis=1), 2, axis=2)


def body(latents, timesteps, time_table, conv_fine, conv_coarse, lift, cotangent):
    count, tile_rows, tile_cols, chans = latents.shape
    table_rows = time_table.shape[0]
    onehot = (timesteps[:, None] == jnp.arange(table_rows, dtype=jnp.int32)[None, :]).astype(
        jnp.float32
    )
    embedding = jnp.dot(onehot, time_table, precision=lax.Precision.HIGHEST)
    padded_in = extended(latents, (("row", 1), ("col", 2)), 1)
    pre_fine = (
        forward_taps(padded_in, conv_fine, tile_rows, tile_cols) + embedding[:, None, None, :]
    )
    hidden = jax.nn.silu(pre_fine).astype(jnp.bfloat16)
    pooled = (0.25 * block_sum(hidden)).astype(jnp.bfloat16)
    half_rows, half_cols = (tile_rows // 2, tile_cols // 2)
    padded_pool = extended(pooled, (("row", 1), ("col", 2)), 1)
    pre_coarse = forward_taps(padded_pool, conv_coarse, half_rows, half_cols)
    coarse_act = jax.nn.silu(pre_coarse).astype(jnp.bfloat16)
    up_grad = block_sum(cotangent)
    lift_part = jnp.einsum(
        "bhwc,bhwd->cd", coarse_act.astype(jnp.float32), up_grad, precision=lax.Precision.HIGHEST
    )
    coarse_back = jnp.einsum("bhwd,cd->bhwc", up_grad, lift, precision=lax.Precision.HIGHEST)
    grad_coarse = (coarse_back * silu_slope(pre_coarse)).astype(jnp.bfloat16)
    padded_grad = extended(grad_coarse, (("row", 1), ("col", 2)), 1)
    coarse_part = weight_taps(padded_pool, grad_coarse, half_rows, half_cols)
    pooled_grad = back_taps(padded_grad, conv_coarse, half_rows, half_cols)
    hidden_grad = cotangent.astype(jnp.float32) + 0.25 * upsample(pooled_grad)
    grad_fine = (hidden_grad * silu_slope(pre_fine)).astype(jnp.bfloat16)
    fine_part = weight_taps(padded_in, grad_fine, tile_rows, tile_cols)
    latent_sum = grad_fine.astype(jnp.float32).sum(axis=(1, 2))
    table_part = jnp.dot(onehot.T, latent_sum, precision=lax.Precision.HIGHEST)
    padded_fine = extended(grad_fine, (("row", 1), ("col", 2)), 1)
    latent_grad = back_taps(padded_fine, conv_fine, tile_rows, tile_cols)
    lift_total, coarse_total, fine_total, table_total = lax.psum(
        (lift_part, coarse_part, fine_part, table_part), ("row", "col")
    )
    factor = 1.0 / math.sqrt(
        count * tile_rows * tile_cols * lax.axis_size("row") * lax.axis_size("col")
    )
    return (
        latent_grad,
        factor * fine_total,
        factor * coarse_total,
        factor * lift_total,
        factor * table_total,
    )


def solution(mesh):
    in_specs = (P(None, "row", "col", None), P(), P(), P(), P(), P(), P(None, "row", "col", None))
    out_specs = (P(None, "row", "col", None), P(), P(), P(), P())
    return jax.shard_map(body, mesh=mesh, in_specs=in_specs, out_specs=out_specs, check_vma=False)
```

profile of v0, /device:TPU:1, one launch (start us, length us, event | category | flops | bytes accessed | tf_op | source)
XLA Modules:
  0.0 325.5 jit_solution(9141574509836222060)
XLA Ops:
  7.2 0.8 fusion.207
  8.1 3.9 %collective-permute-start = (bf16[2,1,64,128]{3,2,1,0:T(8,128)(2,1)S(1)}, bf16[2,1,64,128]{3,2,1,0:T(8,128)(2,1)S(1)}, u32[]{:S(2)}, u32[]{:S(2)}) collective-permute-start(bf16[2,1,64,128]{3,2,1,0:T(8,128)(2,1)S(1)} %get-tuple-element.22), channel_id=1, source_target_pairs={{0,16},{16,32},{32,48},{48,64},{64,80},{80,96},{96,112},{1,17},{17... | collective-permute-start | bytes 98312 | tf_op jit(solution)/shard_map/ppermute | solution.py:16
  12.0 1.3 collective-permute-start.1
  13.3 4.3 %fusion.152 = f32[2,64,64,128]{3,2,1,0:T(8,128)} fusion(bf16[2,64,64,128]{3,2,1,0:T(8,128)(2,1)} %param.7, bf16[3,3,128,128]{3,2,1,0:T(8,128)(2,1)} %param.10), kind=kOutput, calls=%fused_computation.217 | convolution fusion | flops 268435456 | bytes 6324224 | tf_op jit(solution)/shard_map/bhwc,cd->bhwd/dot_general | solution.py:32
  17.9 6.3 %reduce_sum.27 = f32[2,32,32,128]{3,2,1,0:T(8,128)} reduce(bf16[2,32,2,32,2,128]{5,4,3,2,1,0:T(2,128)(2,1)} %bitcast.358, f32[]{:T(128)} %constant.4.clone.1), dimensions={2,4}, to_apply=%region_0.1 | reduce | flops 786432 | bytes 3145732 | tf_op jit(solution)/shard_map/reduce_sum | solution.py:71
  24.2 1.5 constant_dynamic-update-slice_fusion.3
  25.9 5.7 %collective-permute-start.2 = (bf16[2,66,1,128]{3,2,1,0:T(2,128)(2,1)S(1)}, bf16[2,66,1,128]{3,2,1,0:T(2,128)(2,1)S(1)}, u32[]{:S(2)}, u32[]{:S(2)}) collective-permute-start(bf16[2,66,1,128]{3,2,1,0:T(2,128)(2,1)S(1)} %get-tuple-element.16), channel_id=1, source_target_pairs={{0,1},{1,2},{2,3},{3,4},{4,5},{5,6},{6,7},{7,8},{8,9},{9,10},{10,1... | collective-permute-start | bytes 101384 | tf_op jit(solution)/shard_map/ppermute | solution.py:16
  31.5 2.1 collective-permute-start.3
  33.7 2.7 fusion.160
  36.4 2.7 fusion.142
  39.1 2.7 fusion.139
  41.9 2.6 fusion.148
  44.5 2.7 fusion.145
  47.2 2.8 fusion.155
  50.0 2.8 fusion.33
  53.5 13.0 %multiply_convert_fusion.1 = (bf16[2,64,64,128]{3,2,1,0:T(8,128)(2,1)S(1)}, f32[2,64,64,128]{3,2,1,0:T(8,128)}) fusion(f32[2,128]{1,0:T(2,128)S(1)} %fusion.181, bf16[3,3,128,128]{3,2,1,0:T(8,128)(2,1)S(1)} %copy-done.14, bf16[2,66,1,128]{3,2,1,0:T(2,128)(2,1)S(1)} %collective-permute-done.3, bf16[2,66,64,128]{3,2,1,0:T(8,128)(2,1)S(1)} %get-tuple-element.38, ...), kind=kOutput, calls=%fused_computation.4 | convolution fusion | flops 287309824 | bytes 42109952 | tf_op jit(solution)/shard_map/bhwc,cd->bhwd/dot_general | solution.py:32
  66.5 3.5 %convert_reduce_fusion = f32[2,32,32,128]{3,2,1,0:T(8,128)S(1)} fusion(bf16[2,32,2,32,2,128]{5,4,3,2,1,0:T(2,128)(2,1)S(1)} %bitcast.359), kind=kLoop, calls=%fused_computation | loop fusion | flops 1835008 | bytes 3145728 | tf_op jit(solution)/shard_map/reduce_sum | solution.py:71
  70.1 4.3 %collective-permute-start.4 = (bf16[2,1,32,128]{3,2,1,0:T(8,128)(2,1)S(1)}, bf16[2,1,32,128]{3,2,1,0:T(8,128)(2,1)S(1)}, u32[]{:S(2)}, u32[]{:S(2)}) collective-permute-start(bf16[2,1,32,128]{3,2,1,0:T(8,128)(2,1)S(1)} %get-tuple-element.34), channel_id=1, source_target_pairs={{0,16},{16,32},{32,48},{48,64},{64,80},{80,96},{96,112},{1,17},{17... | collective-permute-start | bytes 49160 | tf_op jit(solution)/shard_map/ppermute | solution.py:16
  74.4 1.3 collective-permute-start.5
  76.2 2.7 collective-permute-done.5
  79.0 6.6 %collective-permute-start.6 = (bf16[2,34,1,128]{3,2,1,0:T(2,128)(2,1)S(1)}, bf16[2,34,1,128]{3,2,1,0:T(2,128)(2,1)S(1)}, u32[]{:S(2)}, u32[]{:S(2)}) collective-permute-start(bf16[2,34,1,128]{3,2,1,0:T(2,128)(2,1)S(1)} %get-tuple-element.33), channel_id=1, source_target_pairs={{0,1},{1,2},{2,3},{3,4},{4,5},{5,6},{6,7},{7,8},{8,9},{9,10},{10,1... | collective-permute-start | bytes 52232 | tf_op jit(solution)/shard_map/ppermute | solution.py:16
  85.5 2.2 collective-permute-start.7
  88.6 3.7 %collective-permute-done.7 = bf16[2,34,1,128]{3,2,1,0:T(2,128)(2,1)S(1)} collective-permute-done((bf16[2,34,1,128]{3,2,1,0:T(2,128)(2,1)S(1)}, bf16[2,34,1,128]{3,2,1,0:T(2,128)(2,1)S(1)}, u32[]{:S(2)}, u32[]{:S(2)}) %collective-permute-start.7) | collective-permute-done | bytes 17440 | tf_op jit(solution)/shard_map/ppermute | solution.py:17
  94.9 0.9 add_add_fusion.2
  96.1 2.2 multiply_convert_fusion.3
  99.1 2.3 convolution_bitcast_fusion.2
  103.7 3.1 collective-permute-start.8
  106.8 1.3 collective-permute-start.9
  108.9 3.3 %collective-permute-done.9 = bf16[2,1,32,256]{3,2,1,0:T(8,128)(2,1)S(1)} collective-permute-done((bf16[2,1,32,256]{3,2,1,0:T(8,128)(2,1)S(1)}, bf16[2,1,32,256]{3,2,1,0:T(8,128)(2,1)S(1)}, u32[]{:S(2)}, u32[]{:S(2)}) %collective-permute-start.9) | collective-permute-done | bytes 32800 | tf_op jit(solution)/shard_map/ppermute | solution.py:17
  112.3 3.1 collective-permute-start.10
  115.4 2.4 collective-permute-start.11
  118.7 3.9 %collective-permute-done.11 = bf16[2,34,1,256]{3,2,1,0:T(2,128)(2,1)S(1)} collective-permute-done((bf16[2,34,1,256]{3,2,1,0:T(2,128)(2,1)S(1)}, bf16[2,34,1,256]{3,2,1,0:T(2,128)(2,1)S(1)}, u32[]{:S(2)}, u32[]{:S(2)}) %collective-permute-start.11) | collective-permute-done | bytes 34848 | tf_op jit(solution)/shard_map/ppermute | solution.py:17
  122.6 0.8 maximum_maximum_fusion.1
  126.4 3.7 %broadcast_in_dim.10 = f32[2,64,32,2,128]{4,3,2,1,0:T(2,128)} broadcast(f32[2,64,32,128]{3,2,1,0:T(8,128)S(1)} %bitcast.360), dimensions={0,1,2,4} | broadcast | bytes 6291456 | tf_op jit(solution)/shard_map/broadcast_in_dim | solution.py:76
  130.1 4.6 %convert_reduce_fusion.1 = (f32[2,128]{1,0:T(2,128)S(1)}, bf16[2,64,64,128]{3,2,1,0:T(8,128)(2,1)S(1)}) fusion(f32[2,64,64,128]{3,2,1,0:T(8,128)} %get-tuple-element.41, f32[2,64,64,128]{3,2,1,0:T(8,128)} %bitcast.357, bf16[2,64,64,128]{3,2,1,0:T(8,128)(2,1)S(1)} %copy-done.9), kind=kLoop, calls=%fused_computation.1 | loop fusion | flops 13631232 | bytes 12583936 | tf_op jit(solution)/shard_map/reduce_sum | solution.py:108
  134.8 2.7 fusion.150
  137.4 0.9 fusion.56
  139.8 0.9 fusion.55
  140.7 0.9 fusion.54
  142.3 0.8 fusion.53
  143.1 0.9 fusion.52
  144.0 0.9 fusion.49
  145.6 0.8 fusion.50
  146.4 5.7 %collective-permute-start.12 = (bf16[2,1,64,128]{3,2,1,0:T(8,128)(2,1)S(1)}, bf16[2,1,64,128]{3,2,1,0:T(8,128)(2,1)S(1)}, u32[]{:S(2)}, u32[]{:S(2)}) collective-permute-start(bf16[2,1,64,128]{3,2,1,0:T(8,128)(2,1)S(1)} %get-tuple-element.17), channel_id=1, source_target_pairs={{0,16},{16,32},{32,48},{48,64},{64,80},{80,96},{96,112},{1,17},{17... | collective-permute-start | bytes 98312 | tf_op jit(solution)/shard_map/ppermute | solution.py:16
  152.1 1.3 collective-permute-start.13
  153.4 0.9 fusion.47
  154.3 1.5 fusion.180
  155.9 1.2 collective-permute-done.13
  157.2 3.0 collective-permute-start.14
  160.2 1.9 collective-permute-start.15
  162.1 2.8 fusion
  164.9 2.7 fusion.4
  168.1 1.7 pad_maximum_fusion
  169.7 2.7 fusion.16
  172.5 2.6 fusion.20
  175.1 2.8 fusion.18
  177.9 2.8 fusion.22
  180.7 2.7 fusion.24
  183.5 0.9 copy-done.5
  184.4 11.6 %add_add_fusion = f32[2,64,64,128]{3,2,1,0:T(8,128)} fusion(f32[2,64,64,128]{3,2,1,0:T(8,128)} %fusion.4, f32[2,64,64,128]{3,2,1,0:T(8,128)} %fusion.16, f32[2,64,64,128]{3,2,1,0:T(8,128)} %fusion.18, f32[2,64,64,128]{3,2,1,0:T(8,128)S(1)} %copy-done.5, f32[2,64,64,128]{3,2,1,0:T(8,128)} %fusion.20, f32[2,64,64,128]{3,2,1,0:T(8,128)} %fusion.22, ...), kind=kOutput, calls=%fused_computation.2 | convolution fusion | flops 276824064 | bytes 39878656 | tf_op jit(solution)/shard_map/bhwd,cd->bhwc/dot_general | solution.py:46
  196.0 117.5 %all-reduce.3.cloned.1.call-done = (f32[3,3,128,128]{3,2,1,0:T(8,128)}, f32[3,3,128,256]{3,2,1,0:T(8,128)}, f32[256,128]{1,0:T(8,128)}, f32[1000,128]{1,0:T(8,128)}) async-done(((f32[3,3,128,128]{3,2,1,0:T(8,128)}, f32[3,3,128,256]{3,2,1,0:T(8,128)}, f32[256,128]{1,0:T(8,128)}, f32[1000,128]{1,0:T(8,128)}), (f32[3,3,128,128]{3,2,1,0:T(8,128)}, f32[3,3,128,256]{3,2,1,0:T(8,128)}, f32[256,128]{1,0:T(8,128)}, ...) | async-done | bytes 2412560 | tf_op jit(solution)/shard_map/psum | solution.py:112
  313.6 2.5 broadcast_multiply_fusion
  316.1 0.9 broadcast_multiply_fusion.1
  316.9 0.8 broadcast_multiply_fusion.2
  (99 shorter events, 17.5 us)
Async XLA Ops:
  7.2 10.4 %copy-start = (f32[1000,128]{1,0:T(8,128)S(1)}, f32[1000,128]{1,0:T(8,128)}, u32[]{:S(2)}) copy-start(f32[1000,128]{1,0:T(8,128)} %param.9) | copy-start | bytes 1536004
  7.2 306.4 %all-reduce.3.cloned.1.call-start = ((), (), s32[]{:S(2)}) async-start(), calls=%async_computation | async-start | bytes 4825088 | tf_op jit(solution)/shard_map/psum | solution.py:112
  8.1 16.1 %collective-permute-start = (bf16[2,1,64,128]{3,2,1,0:T(8,128)(2,1)S(1)}, bf16[2,1,64,128]{3,2,1,0:T(8,128)(2,1)S(1)}, u32[]{:S(2)}, u32[]{:S(2)}) collective-permute-start(bf16[2,1,64,128]{3,2,1,0:T(8,128)(2,1)S(1)} %get-tuple-element.22), channel_id=1, source_target_pairs={{0,16},{16,32},{32,48},{48,64},{64,80},{80,96},{96,112},{1,17},{17... | collective-permute-start | bytes 98312 | tf_op jit(solution)/shard_map/ppermute | solution.py:16
  12.0 5.6 %copy-start.21 = (s32[2]{0:T(128)S(1)}, s32[2]{0:T(128)}, u32[]{:S(2)}) copy-start(s32[2]{0:T(128)} %param.8) | copy-start | bytes 28
  12.0 13.7 %collective-permute-start.1 = (bf16[2,1,64,128]{3,2,1,0:T(8,128)(2,1)S(1)}, bf16[2,1,64,128]{3,2,1,0:T(8,128)(2,1)S(1)}, u32[]{:S(2)}, u32[]{:S(2)}) collective-permute-start(bf16[2,1,64,128]{3,2,1,0:T(8,128)(2,1)S(1)} %get-tuple-element.23), channel_id=1, source_target_pairs={{16,0},{32,16},{48,32},{64,48},{80,64},{96,80},{112,96},{17,1},{33... | collective-permute-start | bytes 98312 | tf_op jit(solution)/shard_map/ppermute | solution.py:17
  17.6 6.6 %copy-start.2 = (bf16[2,64,64,128]{3,2,1,0:T(8,128)(2,1)S(1)}, bf16[2,64,64,128]{3,2,1,0:T(8,128)(2,1)}, u32[]{:S(2)}) copy-start(bf16[2,64,64,128]{3,2,1,0:T(8,128)(2,1)} %param.7) | copy-start | bytes 6291460
  24.2 9.5 %copy-start.14 = (bf16[3,3,128,128]{3,2,1,0:T(8,128)(2,1)S(1)}, bf16[3,3,128,128]{3,2,1,0:T(8,128)(2,1)}, u32[]{:S(2)}) copy-start(bf16[3,3,128,128]{3,2,1,0:T(8,128)(2,1)} %param.10) | copy-start | bytes 884740
  25.7 10.7 %copy-start.11 = (bf16[2,65,64,128]{3,2,1,0:T(8,128)(2,1)}, bf16[2,65,64,128]{3,2,1,0:T(8,128)(2,1)S(1)}, u32[]{:S(2)}) copy-start(bf16[2,65,64,128]{3,2,1,0:T(8,128)(2,1)S(1)} %get-tuple-element.19) | copy-start | bytes 6389764
  25.7 10.6 %copy-start.7 = (bf16[2,65,64,128]{3,2,1,0:T(8,128)(2,1)}, bf16[2,65,64,128]{3,2,1,0:T(8,128)(2,1)S(1)}, u32[]{:S(2)}) copy-start(bf16[2,65,64,128]{3,2,1,0:T(8,128)(2,1)S(1)} %get-tuple-element.39) | copy-start | bytes 6389764
  25.9 13.3 %collective-permute-start.2 = (bf16[2,66,1,128]{3,2,1,0:T(2,128)(2,1)S(1)}, bf16[2,66,1,128]{3,2,1,0:T(2,128)(2,1)S(1)}, u32[]{:S(2)}, u32[]{:S(2)}) collective-permute-start(bf16[2,66,1,128]{3,2,1,0:T(2,128)(2,1)S(1)} %get-tuple-element.16), channel_id=1, source_target_pairs={{0,1},{1,2},{2,3},{3,4},{4,5},{5,6},{6,7},{7,8},{8,9},{9,10},{10,1... | collective-permute-start | bytes 101384 | tf_op jit(solution)/shard_map/ppermute | solution.py:16
  31.5 13.0 %collective-permute-start.3 = (bf16[2,66,1,128]{3,2,1,0:T(2,128)(2,1)S(1)}, bf16[2,66,1,128]{3,2,1,0:T(2,128)(2,1)S(1)}, u32[]{:S(2)}, u32[]{:S(2)}) collective-permute-start(bf16[2,66,1,128]{3,2,1,0:T(2,128)(2,1)S(1)} %get-tuple-element.15), channel_id=1, source_target_pairs={{1,0},{2,1},{3,2},{4,3},{5,4},{6,5},{7,6},{8,7},{9,8},{10,9},{11,1... | collective-permute-start | bytes 101384 | tf_op jit(solution)/shard_map/ppermute | solution.py:17
  50.0 3.5 %copy-start.4 = (f32[2,64,64,128]{3,2,1,0:T(8,128)S(1)}, f32[2,64,64,128]{3,2,1,0:T(8,128)}, u32[]{:S(2)}) copy-start(f32[2,64,64,128]{3,2,1,0:T(8,128)} %fusion.152) | copy-start | bytes 12582916
  66.5 9.2 %copy-start.10 = (bf16[3,3,128,256]{3,2,1,0:T(8,128)(2,1)S(1)}, bf16[3,3,128,256]{3,2,1,0:T(8,128)(2,1)}, u32[]{:S(2)}) copy-start(bf16[3,3,128,256]{3,2,1,0:T(8,128)(2,1)} %param.11) | copy-start | bytes 1769476
  70.1 6.0 %collective-permute-start.4 = (bf16[2,1,32,128]{3,2,1,0:T(8,128)(2,1)S(1)}, bf16[2,1,32,128]{3,2,1,0:T(8,128)(2,1)S(1)}, u32[]{:S(2)}, u32[]{:S(2)}) collective-permute-start(bf16[2,1,32,128]{3,2,1,0:T(8,128)(2,1)S(1)} %get-tuple-element.34), channel_id=1, source_target_pairs={{0,16},{16,32},{32,48},{48,64},{64,80},{80,96},{96,112},{1,17},{17... | collective-permute-start | bytes 49160 | tf_op jit(solution)/shard_map/ppermute | solution.py:16
  74.4 4.5 %collective-permute-start.5 = (bf16[2,1,32,128]{3,2,1,0:T(8,128)(2,1)S(1)}, bf16[2,1,32,128]{3,2,1,0:T(8,128)(2,1)S(1)}, u32[]{:S(2)}, u32[]{:S(2)}) collective-permute-start(bf16[2,1,32,128]{3,2,1,0:T(8,128)(2,1)S(1)} %get-tuple-element.35), channel_id=1, source_target_pairs={{16,0},{32,16},{48,32},{64,48},{80,64},{96,80},{112,96},{17,1},{33... | collective-permute-start | bytes 49160 | tf_op jit(solution)/shard_map/ppermute | solution.py:17
  79.0 9.6 %collective-permute-start.6 = (bf16[2,34,1,128]{3,2,1,0:T(2,128)(2,1)S(1)}, bf16[2,34,1,128]{3,2,1,0:T(2,128)(2,1)S(1)}, u32[]{:S(2)}, u32[]{:S(2)}) collective-permute-start(bf16[2,34,1,128]{3,2,1,0:T(2,128)(2,1)S(1)} %get-tuple-element.33), channel_id=1, source_target_pairs={{0,1},{1,2},{2,3},{3,4},{4,5},{5,6},{6,7},{7,8},{8,9},{9,10},{10,1... | collective-permute-start | bytes 52232 | tf_op jit(solution)/shard_map/ppermute | solution.py:16
  85.5 6.8 %collective-permute-start.7 = (bf16[2,34,1,128]{3,2,1,0:T(2,128)(2,1)S(1)}, bf16[2,34,1,128]{3,2,1,0:T(2,128)(2,1)S(1)}, u32[]{:S(2)}, u32[]{:S(2)}) collective-permute-start(bf16[2,34,1,128]{3,2,1,0:T(2,128)(2,1)S(1)} %get-tuple-element.32), channel_id=1, source_target_pairs={{1,0},{2,1},{3,2},{4,3},{5,4},{6,5},{7,6},{8,7},{9,8},{10,9},{11,1... | collective-permute-start | bytes 52232 | tf_op jit(solution)/shard_map/ppermute | solution.py:17
  94.9 1.2 copy-start.16
  94.9 1.2 copy-start.22
  103.7 5.1 %collective-permute-start.8 = (bf16[2,1,32,256]{3,2,1,0:T(8,128)(2,1)S(1)}, bf16[2,1,32,256]{3,2,1,0:T(8,128)(2,1)S(1)}, u32[]{:S(2)}, u32[]{:S(2)}) collective-permute-start(bf16[2,1,32,256]{3,2,1,0:T(8,128)(2,1)S(1)} %get-tuple-element.28), channel_id=1, source_target_pairs={{0,16},{16,32},{32,48},{48,64},{64,80},{80,96},{96,112},{1,17},{17... | collective-permute-start | bytes 98312 | tf_op jit(solution)/shard_map/ppermute | solution.py:16
  106.8 5.4 %collective-permute-start.9 = (bf16[2,1,32,256]{3,2,1,0:T(8,128)(2,1)S(1)}, bf16[2,1,32,256]{3,2,1,0:T(8,128)(2,1)S(1)}, u32[]{:S(2)}, u32[]{:S(2)}) collective-permute-start(bf16[2,1,32,256]{3,2,1,0:T(8,128)(2,1)S(1)} %get-tuple-element.29), channel_id=1, source_target_pairs={{16,0},{32,16},{48,32},{64,48},{80,64},{96,80},{112,96},{17,1},{33... | collective-permute-start | bytes 98312 | tf_op jit(solution)/shard_map/ppermute | solution.py:17
  108.8 9.9 %copy-start.13 = (f32[9,128,256]{2,1,0:T(8,128)}, f32[9,128,256]{2,1,0:T(8,128)S(1)}, u32[]{:S(2)}) copy-start(f32[9,128,256]{2,1,0:T(8,128)S(1)} %fusion.39) | copy-start | bytes 3538948
  112.3 6.4 %collective-permute-start.10 = (bf16[2,34,1,256]{3,2,1,0:T(2,128)(2,1)S(1)}, bf16[2,34,1,256]{3,2,1,0:T(2,128)(2,1)S(1)}, u32[]{:S(2)}, u32[]{:S(2)}) collective-permute-start(bf16[2,34,1,256]{3,2,1,0:T(2,128)(2,1)S(1)} %get-tuple-element.26), channel_id=1, source_target_pairs={{0,1},{1,2},{2,3},{3,4},{4,5},{5,6},{6,7},{7,8},{8,9},{9,10},{10,1... | collective-permute-start | bytes 104456 | tf_op jit(solution)/shard_map/ppermute | solution.py:16
  115.4 7.1 %collective-permute-start.11 = (bf16[2,34,1,256]{3,2,1,0:T(2,128)(2,1)S(1)}, bf16[2,34,1,256]{3,2,1,0:T(2,128)(2,1)S(1)}, u32[]{:S(2)}, u32[]{:S(2)}) collective-permute-start(bf16[2,34,1,256]{3,2,1,0:T(2,128)(2,1)S(1)} %get-tuple-element.27), channel_id=1, source_target_pairs={{1,0},{2,1},{3,2},{4,3},{5,4},{6,5},{7,6},{8,7},{9,8},{10,9},{11,1... | collective-permute-start | bytes 104456 | tf_op jit(solution)/shard_map/ppermute | solution.py:17
  126.4 3.7 %copy-start.9 = (bf16[2,64,64,128]{3,2,1,0:T(8,128)(2,1)S(1)}, bf16[2,64,64,128]{3,2,1,0:T(8,128)(2,1)}, u32[]{:S(2)}) copy-start(bf16[2,64,64,128]{3,2,1,0:T(8,128)(2,1)} %param.13) | copy-start | bytes 6291460
  130.1 4.7 %copy-start.15 = (bf16[3,3,128,128]{3,2,1,0:T(8,128)(2,1)S(1)}, bf16[3,3,128,128]{3,2,1,0:T(8,128)(2,1)}, u32[]{:S(2)}) copy-start(bf16[3,3,128,128]{3,2,1,0:T(8,128)(2,1)} %param.10) | copy-start | bytes 884740
  137.4 1.6 copy-start.12
  140.7 1.6 copy-start.3
  144.0 1.6 copy-start.8
  146.4 9.5 %collective-permute-start.12 = (bf16[2,1,64,128]{3,2,1,0:T(8,128)(2,1)S(1)}, bf16[2,1,64,128]{3,2,1,0:T(8,128)(2,1)S(1)}, u32[]{:S(2)}, u32[]{:S(2)}) collective-permute-start(bf16[2,1,64,128]{3,2,1,0:T(8,128)(2,1)S(1)} %get-tuple-element.17), channel_id=1, source_target_pairs={{0,16},{16,32},{32,48},{48,64},{64,80},{80,96},{96,112},{1,17},{17... | collective-permute-start | bytes 98312 | tf_op jit(solution)/shard_map/ppermute | solution.py:16
  152.1 4.9 %collective-permute-start.13 = (bf16[2,1,64,128]{3,2,1,0:T(8,128)(2,1)S(1)}, bf16[2,1,64,128]{3,2,1,0:T(8,128)(2,1)S(1)}, u32[]{:S(2)}, u32[]{:S(2)}) collective-permute-start(bf16[2,1,64,128]{3,2,1,0:T(8,128)(2,1)S(1)} %get-tuple-element.18), channel_id=1, source_target_pairs={{16,0},{32,16},{48,32},{64,48},{80,64},{96,80},{112,96},{17,1},{33... | collective-permute-start | bytes 98312 | tf_op jit(solution)/shard_map/ppermute | solution.py:17
  154.3 1.5 copy-start.18
  157.2 10.4 %collective-permute-start.14 = (bf16[2,66,1,128]{3,2,1,0:T(2,128)(2,1)S(1)}, bf16[2,66,1,128]{3,2,1,0:T(2,128)(2,1)S(1)}, u32[]{:S(2)}, u32[]{:S(2)}) collective-permute-start(bf16[2,66,1,128]{3,2,1,0:T(2,128)(2,1)S(1)} %get-tuple-element.14), channel_id=1, source_target_pairs={{0,1},{1,2},{2,3},{3,4},{4,5},{5,6},{6,7},{7,8},{8,9},{9,10},{10,1... | collective-permute-start | bytes 101384 | tf_op jit(solution)/shard_map/ppermute | solution.py:16
  160.2 7.9 %collective-permute-start.15 = (bf16[2,66,1,128]{3,2,1,0:T(2,128)(2,1)S(1)}, bf16[2,66,1,128]{3,2,1,0:T(2,128)(2,1)S(1)}, u32[]{:S(2)}, u32[]{:S(2)}) collective-permute-start(bf16[2,66,1,128]{3,2,1,0:T(2,128)(2,1)S(1)} %get-tuple-element.13), channel_id=1, source_target_pairs={{1,0},{2,1},{3,2},{4,3},{5,4},{6,5},{7,6},{8,7},{9,8},{10,9},{11,1... | collective-permute-start | bytes 101384 | tf_op jit(solution)/shard_map/ppermute | solution.py:17
  177.9 5.6 %copy-start.6 = (f32[2,64,64,128]{3,2,1,0:T(8,128)S(1)}, f32[2,64,64,128]{3,2,1,0:T(8,128)}, u32[]{:S(2)}) copy-start(f32[2,64,64,128]{3,2,1,0:T(8,128)} %fusion) | copy-start | bytes 12582916
  180.7 3.7 %copy-start.5 = (f32[2,64,64,128]{3,2,1,0:T(8,128)S(1)}, f32[2,64,64,128]{3,2,1,0:T(8,128)}, u32[]{:S(2)}) copy-start(f32[2,64,64,128]{3,2,1,0:T(8,128)} %fusion.150) | copy-start | bytes 12582916
  313.6 2.5 copy-start.17
  313.6 3.4 %copy-start.19 = (f32[1000,128]{1,0:T(8,128)S(1)}, f32[1000,128]{1,0:T(8,128)}, u32[]{:S(2)}) copy-start(f32[1000,128]{1,0:T(8,128)} %get-tuple-element.8) | copy-start | bytes 1536004
  313.6 4.9 %copy-start.1 = (f32[1000,128]{1,0:T(8,128)S(1)}, f32[1000,128]{1,0:T(8,128)}, u32[]{:S(2)}) copy-start(f32[1000,128]{1,0:T(8,128)} %param.9) | copy-start | bytes 1536004
  313.6 4.2 %copy-start.20 = (f32[256,128]{1,0:T(8,128)S(1)}, f32[256,128]{1,0:T(8,128)}, u32[]{:S(2)}) copy-start(f32[256,128]{1,0:T(8,128)} %get-tuple-element.7) | copy-start | bytes 393220
Sparse Core Ops, SparseCore 0:
  156.0 157.5 all-reduce.2
where the time goes:
time: 331 us; the launch traced here: 326 us
  waiting for transfers between devices  133 us (40%)
  matrix products  95.3 us (29%)
  starting transfers between devices  49.2 us (15%)
  other arithmetic  22.6 us (7%)
  between operations  14.9 us (5%)
  local copies, waits for them, and re-layouts  10.6 us (3%)
    psum x1, waiting for transfers between devices, body(): lax.psum((lift_part, coarse_part, fine_part, table_part), ('row', 'col'))  118 us
    dot_general x18, matrix products, forward_taps(): jnp.einsum('bhwc,cd->bhwd', window, kernel[row_tap, col_tap], preferred_e...  40.6 us
    dot_general x18, matrix products, back_taps(): jnp.einsum('bhwd,cd->bhwc', window, kernel[2 - row_tap, 2 - col_tap], pre...  37.5 us
    ppermute x8, starting transfers between devices, extended(): before = lax.ppermute(last, axis, up)  35.4 us
    ppermute x8, waiting for transfers between devices, extended(): after = lax.ppermute(first, axis, down)  15.3 us
    ppermute x8, starting transfers between devices, extended(): after = lax.ppermute(first, axis, down)  13.8 us
    dot_general x18, matrix products, weight_taps(): jnp.einsum('bhwc,bhwd->cd', window, grad_in, preferred_element_type=jnp.f...  11 us
    reduce_sum x2, other arithmetic, block_sum(): return field_in.astype(jnp.float32).reshape(count, tall // 2, 2, broad //...  9.76 us
  transfers between devices with their start and end apart: 17, of which 7 were waited for; matrix products, arithmetic and copies ran while one was open for 19% of the time, Pallas kernels for 0%

commit v1 on v0

v1 whole, which is shorter than its diff:
```python
import functools
import math

import jax
import jax.numpy as jnp
from jax import lax
from jax.experimental import pallas as pl
from jax.experimental.pallas import tpu as pltpu
from jax.sharding import PartitionSpec as P

MESH = pl.DeviceIdType.MESH
f32 = jnp.float32
bf16 = jnp.bfloat16


def dot(a, b):
    return jnp.dot(a, b, preferred_element_type=f32)


def sigmoid(v):
    return 0.5 + 0.5 * jnp.tanh(0.5 * v)


def shifted(v, column, step):
    n = v.shape[1]
    ids = lax.broadcasted_iota(jnp.int32, v.shape, 1)
    edge = 0 if step == 1 else n - 1
    return jnp.where(ids == edge, column[:, None, :], pltpu.roll(v, step % n, 1))


def kernel(
    sizes,
    times, lat_in, cot_in, table_in, fine_in, coarse_in, lift_in,
    grad_out, fine_out, coarse_out, lift_out, table_out,
    lat, cot, table, kfine, kcoarse, lift, wide,
    w_fwd, w_back, wc_back, lift_hi, lift_lo,
    V, C2, SL, PO, UG, ACT, GC, G, VT, PT, OUT,
    sc_v, rc_v, sc_p, rc_p, sc_c, rc_c, sc_g, rc_g,
    a_send, a_r1, a_s2, a_r2, a_t, a_g, a_f,
    b_send, b_r1, b_s2, b_r2, b_t, b_g, b_f,
    l_send, l_r1, l_s2, l_r2,
    in_sem, out_sem, h_ssem, h_rsem, a_ssem, a_rsem, b_ssem, b_rsem, l_ssem, l_rsem,
):
    nr, nc, factor = sizes
    row, col = lax.axis_index("row"), lax.axis_index("col")
    up, down = lax.rem(row + nr - 1, nr), lax.rem(row + 1, nr)
    left, right = lax.rem(col + nc - 1, nc), lax.rem(col + 1, nc)
    count, tall, half = C2.shape[0], C2.shape[1], C2.shape[2]
    low = tall // 2
    chans = lat.shape[3]

    barrier = pltpu.get_barrier_semaphore()
    partners = [(lax.rem(row + d, nr), col) for d in range(1, nr)]
    partners += [(row, lax.rem(col + d, nc)) for d in range(1, nc)]
    partners += [(up, left), (up, right), (down, left), (down, right)]
    for who in partners:
        pl.semaphore_signal(barrier, inc=1, device_id=who, device_id_type=MESH)

    loads = {}
    pairs = [(lat_in.at[b], lat.at[b]) for b in range(count)]
    pairs += [(fine_in, kfine), (table_in, table)]
    pairs += [(cot_in.at[b], cot.at[b]) for b in range(count)]
    pairs += [(coarse_in, kcoarse), (lift_in, lift)]
    names = ["lat0", "lat1", "kfine", "table", "cot0", "cot1", "kcoarse", "lift"]
    for at, (src, dst) in enumerate(pairs):
        loads[names[at]] = pltpu.make_async_copy(src, dst, in_sem.at[at])
        loads[names[at]].start()

    def exchange(kind, b, buf, n, lo, hi, sc, rc):
        top, bottom = (row, col), None
        first = (kind * count + b) * 8
        first_col, last_col = sc.at[b, 0], sc.at[b, 1]
        to_left, to_right = rc.at[b, 1], rc.at[b, 0]
        lanes = pl.ds(lo, hi - lo)
        plan = [
            (buf.at[b, 1, :, lanes], buf.at[b, n + 1, :, lanes], (up, col)),
            (buf.at[b, n, :, lanes], buf.at[b, 0, :, lanes], (down, col)),
            (first_col, to_left.at[pl.ds(8, n)], (row, left)),
            (last_col, to_right.at[pl.ds(8, n)], (row, right)),
            (first_col.at[pl.ds(0, 8)], to_left.at[pl.ds(n + 8, 8)], (up, left)),
            (last_col.at[pl.ds(0, 8)], to_right.at[pl.ds(n + 8, 8)], (up, right)),
            (first_col.at[pl.ds(n - 8, 8)], to_left.at[pl.ds(0, 8)], (down, left)),
            (last_col.at[pl.ds(n - 8, 8)], to_right.at[pl.ds(0, 8)], (down, right)),
        ]
        return [
            pltpu.make_async_remote_copy(
                src_ref=src, dst_ref=dst, send_sem=h_ssem.at[first + at], recv_sem=h_rsem.at[first + at],
                device_id=who, device_id_type=MESH)
            for at, (src, dst, who) in enumerate(plan)
        ]

    def send(copies):
        for c in copies:
            c.start()

    def arrive(copies, b, buf, n, lo, hi, rc):
        for c in copies:
            c.wait()
        nothing = jnp.zeros((buf.shape[2], hi - lo), buf.dtype)

        @pl.when(row == 0)
        def _():
            buf[b, 0, :, lo:hi] = nothing
            rc[b, :, 0:8, :] = jnp.zeros((2, 8, rc.shape[3]), f32)

        @pl.when(row == nr - 1)
        def _():
            buf[b, n + 1, :, lo:hi] = nothing
            rc[b, :, n + 8 : n + 16, :] = jnp.zeros((2, 8, rc.shape[3]), f32)

        @pl.when(col == 0)
        def _():
            rc[b, 0] = jnp.zeros(rc.shape[2:], f32)

        @pl.when(col == nc - 1)
        def _():
            rc[b, 1] = jnp.zeros(rc.shape[2:], f32)

    def widen_fine(buf, b, rc):
        before, after = rc[b, 0, 7 : 7 + tall + 2, :], rc[b, 1, 7 : 7 + tall + 2, :]
        odd = buf[b, :, :, 2 * chans : 3 * chans].astype(f32)
        buf[b, :, :, 0:chans] = shifted(odd, before, 1).astype(bf16)
        even = buf[b, :, :, chans : 2 * chans].astype(f32)
        buf[b, :, :, 3 * chans : 4 * chans] = shifted(even, after, -1).astype(bf16)

    def widen_coarse(buf, b, rc):
        wide_by = rc.shape[3]
        before, after = rc[b, 0, 7 : 7 + low + 2, :], rc[b, 1, 7 : 7 + low + 2, :]
        mid = buf[b, :, :, wide_by : 2 * wide_by].astype(f32)
        buf[b, :, :, 0:wide_by] = shifted(mid, before, 1).astype(bf16)
        buf[b, :, :, 2 * wide_by : 3 * wide_by] = shifted(mid, after, -1).astype(bf16)

    def columns_fine(buf, b, sc):
        sc[b, 0] = buf[b, 1 : tall + 1, 0:16, chans : 2 * chans].astype(f32)[:, 0, :]
        sc[b, 1] = buf[b, 1 : tall + 1, half - 16 : half, 2 * chans : 3 * chans].astype(f32)[:, 15, :]

    def columns_coarse(buf, b, sc):
        wide_by = sc.shape[3]
        lanes = slice(wide_by, 2 * wide_by)
        sc[b, 0] = buf[b, 1 : low + 1, 0:16, lanes].astype(f32)[:, 0, :]
        sc[b, 1] = buf[b, 1 : low + 1, half - 16 : half, lanes].astype(f32)[:, 15, :]

    step = 8

    def split_latents(b):
        def one(k, _):
            rows = pl.ds(k * step, step)
            wide[...] = lat[b, rows].astype(f32)
            even, odd = wide[:, pl.ds(0, half, stride=2), :], wide[:, pl.ds(1, half, stride=2), :]
            V[b, pl.ds(k * step + 1, step), :, chans : 3 * chans] = jnp.concatenate([even, odd], -1).astype(bf16)
            return 0

        lax.fori_loop(0, tall // step, one, 0)

    def split_cotangent(b):
        def one(k, _):
            wide[...] = cot[b, pl.ds(k * step, step)].astype(f32)
            even, odd = wide[:, pl.ds(0, half, stride=2), :], wide[:, pl.ds(1, half, stride=2), :]
            C2[b, pl.ds(k * step, step)] = jnp.concatenate([even, odd], -1).astype(bf16)
            total = (even + odd).reshape(step // 2, 2, half, chans).sum(axis=1)
            upper = total.astype(bf16)
            rest = (total - upper.astype(f32)).astype(bf16)
            UG[b, pl.ds(k * (step // 2), step // 2)] = jnp.concatenate([upper, rest], -1)
            return 0

        lax.fori_loop(0, tall // step, one, 0)

    def prepare_forward():
        w_fwd[...] = jnp.zeros(w_fwd.shape, bf16)
        for i in range(3):
            base = i * 4 * chans
            for part in range(2):
                for j in range(3):
                    at = base + (part + j) * chans
                    w_fwd[at : at + chans, part * chans : (part + 1) * chans] = kfine[i, j]

    def prepare_back():
        w_back[...] = jnp.zeros(w_back.shape, bf16)
        for i in range(3):
            for j in range(3):
                turned = kfine[i, j].T
                for part in range(2):
                    at = i * 4 * chans + (part + 2 - j) * chans
                    w_back[at : at + chans, part * chans : (part + 1) * chans] = turned
                at = (i * 3 + 2 - j) * 2 * chans
                wc_back[at : at + 2 * chans, :] = kcoarse[i, j].T

    def prepare_lift():
        turned = lift[...].T
        upper = turned.astype(bf16)
        lift_hi[0:chans, :] = upper
        lift_hi[chans : 2 * chans, :] = upper
        lift_lo[...] = (turned - upper.astype(f32)).astype(bf16)

    flat = step * half

    def forward_fine(b):
        index = times[b]
        embedding = table[pl.ds(index, 1), :]
        embedding = jnp.concatenate([embedding, embedding], -1)

        def one(k, _):
            taps = [V[b, pl.ds(k * step + i, step)].reshape(flat, 4 * chans) for i in range(3)]
            pre = dot(jnp.concatenate(taps, -1), w_fwd[...]) + embedding
            s = sigmoid(pre)
            hidden = pre * s
            SL[b, pl.ds(k * step, step)] = (s + hidden * (1.0 - s)).reshape(step, half, 2 * chans)
            hidden = hidden.astype(bf16).astype(f32).reshape(step // 2, 2, half, 2 * chans).sum(axis=1)
            pooled = 0.25 * (hidden[:, :, :chans] + hidden[:, :, chans:])
            PO[b, pl.ds(k * (step // 2) + 1, step // 2), :, chans : 2 * chans] = pooled.astype(bf16)
            return 0

        lax.fori_loop(0, tall // step, one, 0)

    def forward_coarse(b):
        def one(k, _):
            taps = [PO[b, pl.ds(k * step + i, step)].reshape(flat, 3 * chans) for i in range(3)]
            weights = kcoarse[...].reshape(9 * chans, 2 * chans)
            pre = dot(jnp.concatenate(taps, -1), weights)
            s = sigmoid(pre)
            act = pre * s
            ACT[b, pl.ds(pl.multiple_of(k * flat, flat), flat), :] = act.astype(bf16)
            ug = UG[b, pl.ds(k * step, step)].reshape(flat, 2 * chans)
            back = dot(ug, lift_hi[...]) + dot(ug[:, :chans], lift_lo[...])
            grad = (back * (s + act * (1.0 - s))).astype(bf16)
            GC[b, pl.ds(k * step + 1, step), :, 2 * chans : 4 * chans] = grad.reshape(step, half, 2 * chans)
            return 0

        lax.fori_loop(0, low // step, one, 0)

    def backward_coarse(b):
        def one(k, total):
            taps = [GC[b, pl.ds(k * step + 2 - i, step)].reshape(flat, 6 * chans) for i in range(3)]
            pooled = 0.25 * dot(jnp.concatenate(taps, -1), wc_back[...])
            pooled = pooled.reshape(step, 1, half, chans)
            pooled = jnp.concatenate([pooled, pooled], -1)
            rows = pl.ds(k * 2 * step, 2 * step)
            direct = C2[b, rows].astype(f32).reshape(step, 2, half, 2 * chans)
            slope = SL[b, rows].reshape(step, 2, half, 2 * chans)
            grad = ((direct + pooled) * slope).astype(bf16)
            G[b, pl.ds(k * 2 * step + 1, 2 * step), :, chans : 3 * chans] = grad.reshape(2 * step, half, 2 * chans)
            return total + grad.astype(f32).reshape(2 * flat // 8, 8, 2 * chans).sum(axis=0)

        total = lax.fori_loop(0, low // step, one, jnp.zeros((8, 2 * chans), f32))
        total = total[:, :chans] + total[:, chans:]
        return total.sum(axis=0, keepdims=True)

    def backward_fine(b, part, parts):
        def one(k, _):
            taps = [G[b, pl.ds(k * step + 2 - i, step)].reshape(flat, 4 * chans) for i in range(3)]
            grad = dot(jnp.concatenate(taps, -1), w_back[...]).reshape(step, half, 2 * chans)
            rows = pl.ds(k * step, step)
            OUT[b, rows, pl.ds(0, half, stride=2), :] = grad[:, :, :chans]
            OUT[b, rows, pl.ds(1, half, stride=2), :] = grad[:, :, chans:]
            return 0

        each = tall // step // parts
        lax.fori_loop(part * each, (part + 1) * each, one, 0)
        rows = pl.ds(part * each * step, each * step)
        done = pltpu.make_async_copy(OUT.at[b, rows], grad_out.at[b, rows], out_sem.at[b * parts + part])
        done.start()
        return done

    class Reduce:
        def __init__(self, mine, first, second_in, second, owned, gathered, full, ssem, rsem, items):
            self.refs = mine, first, second_in, second, owned, gathered, full
            self.ssem, self.rsem, self.items = ssem, rsem, items
            self.share = chans // nr

        def copy(self, at, src, dst, who):
            return pltpu.make_async_remote_copy(
                src_ref=src, dst_ref=dst, send_sem=self.ssem.at[at], recv_sem=self.rsem.at[at],
                device_id=who, device_id_type=MESH)

        def rows_of(self, peer):
            return pl.ds(pl.multiple_of(peer * self.share, self.share), self.share)

        def scatter_rows(self, items):
            mine, first = self.refs[:2]
            lo, hi, group = items
            for d in range(1, nr):
                peer = lax.rem(row + d, nr)
                self.copy(group * nr + d, mine.at[pl.ds(lo, hi - lo), self.rows_of(peer)],
                          first.at[d, pl.ds(lo, hi - lo)], (peer, col)).start()

        def sum_rows(self, groups):
            mine, first, second_in = self.refs[:3]
            for lo, hi, group in groups:
                for d in range(1, nr):
                    peer = lax.rem(row + d, nr)
                    self.copy(group * nr + d, mine.at[pl.ds(lo, hi - lo), self.rows_of(peer)],
                              first.at[d, pl.ds(lo, hi - lo)], (peer, col)).wait()
            total = mine[:, self.rows_of(row), :].astype(f32)
            for d in range(1, nr):
                total = total + first[d].astype(f32)
            second_in[...] = total.astype(bf16)

        base2 = property(lambda self: 3 * nr)
        base3 = property(lambda self: 3 * nr + nc)
        base4 = property(lambda self: 3 * nr + 2 * nc)

        def scatter_cols(self):
            _, _, second_in, second = self.refs[:4]
            for d in range(1, nc):
                owner = lax.rem(col + d, nc)

                @pl.when(owner < self.items)
                def _():
                    self.copy(self.base2 + d, second_in.at[owner], second.at[d], (row, owner)).start()

        def sum_cols(self):
            _, _, second_in, second, owned = self.refs[:5]
            for d in range(1, nc):
                owner = lax.rem(col + d, nc)
                c = self.copy(self.base2 + d, second_in.at[0], second.at[d], (row, owner))
                pl.when(owner < self.items)(c.wait_send)
                pl.when(col < self.items)(c.wait_recv)

            @pl.when(col < self.items)
            def _():
                total = second_in[col].astype(f32)
                for d in range(1, nc):
                    total = total + second[d].astype(f32)
                owned[...] = total.astype(bf16)

        def gather_cols(self):
            owned, gathered = self.refs[4:6]

            @pl.when(col < self.items)
            def _():
                gathered[col] = owned[...]
                for d in range(1, nc):
                    peer = lax.rem(col + d, nc)
                    self.copy(self.base3 + d, owned, gathered.at[col], (row, peer)).start()

        def gather_rows(self):
            owned, gathered, full = self.refs[4:]
            for d in range(1, nc):
                source = lax.rem(col + nc - d, nc)
                c = self.copy(self.base3 + d, owned, gathered.at[0], (row, source))
                pl.when(col < self.items)(c.wait_send)
                pl.when(source < self.items)(c.wait_recv)
            full[:, self.rows_of(row), :] = gathered[...]
            for d in range(1, nr):
                peer = lax.rem(row + d, nr)
                self.copy(self.base4 + d, gathered, full.at[:, self.rows_of(row)], (peer, col)).start()

        def finish(self):
            gathered, full = self.refs[5:]
            for d in range(1, nr):
                peer = lax.rem(row + d, nr)
                self.copy(self.base4 + d, gathered, full.at[:, self.rows_of(row)], (peer, col)).wait()

    sum_a = Reduce(a_send, a_r1, a_s2, a_r2, a_t, a_g, a_f, a_ssem, a_rsem, 10)
    sum_b = Reduce(b_send, b_r1, b_s2, b_r2, b_t, b_g, b_f, b_ssem, b_rsem, 9)

    ex_v = [(b, V, tall, chans, 3 * chans) for b in range(count)]
    ex_p = [(b, PO, low, chans, 2 * chans) for b in range(count)]
    ex_c = [(b, GC, low, 2 * chans, 4 * chans) for b in range(count)]
    ex_g = [(b, G, tall, chans, 3 * chans) for b in range(count)]

    loads["lat0"].wait()
    split_latents(0)
    columns_fine(V, 0, sc_v)
    pl.semaphore_wait(barrier, len(partners))
    moving_v = [exchange(0, *ex_v[b], sc_v, rc_v) for b in range(count)]
    send(moving_v[0])
    loads["lat1"].wait()
    split_latents(1)
    columns_fine(V, 1, sc_v)
    send(moving_v[1])
    loads["kfine"].wait()
    prepare_forward()
    loads["table"].wait()
    loads["cot0"].wait()
    split_cotangent(0)

    moving_p = [exchange(1, *ex_p[b], sc_p, rc_p) for b in range(count)]
    for b in range(count):
        arrive(moving_v[b], *ex_v[b], rc_v)
        widen_fine(V, b, rc_v)
        forward_fine(b)
        columns_coarse(PO, b, sc_p)
        send(moving_p[b])

    loads["cot1"].wait()
    split_cotangent(1)
    loads["lift"].wait()
    prepare_lift()
    loads["kcoarse"].wait()

    moving_c = [exchange(2, *ex_c[b], sc_c, rc_c) for b in range(count)]
    for b in range(count):
        arrive(moving_p[b], *ex_p[b], rc_p)
        widen_coarse(PO, b, rc_p)
        forward_coarse(b)
        columns_coarse(GC, b, sc_c)
        send(moving_c[b])

    prepare_back()
    for b in range(count):
        PT[b] = PO[b, 1 : low + 1, :, chans : 2 * chans].reshape(low * half, chans).T
        VT[b] = V[b, 1 : tall + 1, :, chans : 3 * chans].reshape(tall * half, 2 * chans).T
    lifted = jnp.zeros((2 * chans, 2 * chans), f32)
    for b in range(count):
        lifted = lifted + dot(ACT[b].T, UG[b].reshape(low * half, 2 * chans))
    lifted = (lifted[:, :chans] + lifted[:, chans:]).astype(bf16)
    a_send[9, :, 0:chans] = lifted[:chans]
    a_send[9, :, chans : 2 * chans] = lifted[chans:]

    moving_g = [exchange(3, *ex_g[b], sc_g, rc_g) for b in range(count)]
    arrive(moving_c[0], *ex_c[0], rc_c)
    widen_coarse(GC, 0, rc_c)
    sums = [backward_coarse(0)]
    columns_fine(G, 0, sc_g)
    send(moving_g[0])
    arrive(moving_c[1], *ex_c[1], rc_c)
    widen_coarse(GC, 1, rc_c)
    sums.append(backward_coarse(1))
    columns_fine(G, 1, sc_g)
    send(moving_g[1])

    for i in range(3):
        kernel_grad = jnp.zeros((chans, 6 * chans), f32)
        for b in range(count):
            kernel_grad = kernel_grad + dot(PT[b], GC[b, 2 - i : 2 - i + low].reshape(low * half, 6 * chans))
        for j in range(3):
            at = (2 - j) * 2 * chans
            a_send[3 * i + j] = kernel_grad[:, at : at + 2 * chans].astype(bf16)
    a_groups = [(0, 10, 0)]
    sum_a.scatter_rows(a_groups[0])

    l_send[...] = jnp.concatenate(sums + [jnp.zeros((8 - count, chans), f32)], 0)
    l_moving = [
        pltpu.make_async_remote_copy(
            src_ref=l_send, dst_ref=l_r1.at[d], send_sem=l_ssem.at[d], recv_sem=l_rsem.at[d],
            device_id=(lax.rem(row + d, nr), col), device_id_type=MESH)
        for d in range(1, nr)
    ]
    send(l_moving)

    arrive(moving_g[0], *ex_g[0], rc_g)
    widen_fine(G, 0, rc_g)
    arrive(moving_g[1], *ex_g[1], rc_g)
    widen_fine(G, 1, rc_g)

    b_groups = [(3 * i, 3 * i + 3, i) for i in range(3)]
    for i in range(3):
        kernel_grad = jnp.zeros((2 * chans, 4 * chans), f32)
        for b in range(count):
            kernel_grad = kernel_grad + dot(VT[b], G[b, 2 - i : 2 - i + tall].reshape(tall * half, 4 * chans))
        for j in range(3):
            at = (2 - j) * chans
            both = kernel_grad[:chans, at : at + chans] + kernel_grad[chans:, at + chans : at + 2 * chans]
            b_send[3 * i + j] = both.astype(bf16)
        sum_b.scatter_rows(b_groups[i])
        if i == 0:
            sum_a.sum_rows(a_groups)
            sum_a.scatter_cols()
            for c in l_moving:
                c.wait()
            total = l_send[...]
            for d in range(1, nr):
                total = total + l_r1[d]
            l_s2[...] = total
            l_moving2 = [
                pltpu.make_async_remote_copy(
                    src_ref=l_s2, dst_ref=l_r2.at[d], send_sem=l_ssem.at[nr + d], recv_sem=l_rsem.at[nr + d],
                    device_id=(row, lax.rem(col + d, nc)), device_id_type=MESH)
                for d in range(1, nc)
            ]
            send(l_moving2)

    sum_a.sum_cols()
    sum_a.gather_cols()
    stores = [backward_fine(0, 0, 2)]
    sum_b.sum_rows(b_groups)
    sum_b.scatter_cols()
    sum_a.gather_rows()
    stores.append(backward_fine(0, 1, 2))
    sum_b.sum_cols()
    sum_b.gather_cols()
    stores.append(backward_fine(1, 0, 2))
    sum_b.gather_rows()
    stores.append(backward_fine(1, 1, 2))

    for c in l_moving2:
        c.wait()
    total = l_s2[...]
    for d in range(1, nc):
        total = total + l_r2[d]
    total = factor * total
    ids = lax.broadcasted_iota(jnp.int32, table_out.shape, 0)
    placed = jnp.zeros(table_out.shape, f32)
    for b in range(count):
        placed = placed + jnp.where(ids == times[b], total[b : b + 1, :], 0.0)
    table_out[...] = placed

    sum_a.finish()
    for t in range(9):
        coarse_out[t // 3, t % 3] = factor * a_f[t].astype(f32)
    lift_out[0:chans, :] = factor * a_f[9, :, 0:chans].astype(f32)
    lift_out[chans : 2 * chans, :] = factor * a_f[9, :, chans : 2 * chans].astype(f32)
    sum_b.finish()
    for t in range(9):
        fine_out[t // 3, t % 3] = factor * b_f[t].astype(f32)
    for c in stores:
        c.wait()


def solution(mesh):
    nr, nc = mesh.shape["row"], mesh.shape["col"]

    def body(latents, timesteps, time_table, conv_fine, conv_coarse, lift, cotangent):
        count, tall, broad, chans = latents.shape
        half, low = broad // 2, tall // 2
        share = chans // nr
        factor = 1.0 / math.sqrt(count * tall * broad * nr * nc)
        vm = pltpu.VMEM

        def reducer(items, wide):
            return [
                vm((items, chans, wide), bf16),
                vm((nr, items, share, wide), bf16),
                vm((items, share, wide), bf16),
                vm((nc, share, wide), bf16),
                vm((share, wide), bf16),
                vm((items, share, wide), bf16),
                vm((items, chans, wide), bf16),
            ]

        def columns(n, wide):
            return [vm((count, 2, n, wide), f32), vm((count, 2, n + 16, wide), f32)]

        scratch = [
            vm(latents.shape, bf16), vm(cotangent.shape, bf16), vm(time_table.shape, f32),
            vm(conv_fine.shape, bf16), vm(conv_coarse.shape, bf16), vm(lift.shape, f32),
            vm((8, broad, chans), f32),
            vm((12 * chans, 2 * chans), bf16), vm((12 * chans, 2 * chans), bf16), vm((18 * chans, chans), bf16),
            vm((2 * chans, 2 * chans), bf16), vm((chans, 2 * chans), bf16),
            vm((count, tall + 2, half, 4 * chans), bf16),
            vm((count, tall, half, 2 * chans), bf16),
            vm((count, tall, half, 2 * chans), f32),
            vm((count, low + 2, half, 3 * chans), bf16),
            vm((count, low, half, 2 * chans), bf16),
            vm((count, low * half, 2 * chans), bf16),
            vm((count, low + 2, half, 6 * chans), bf16),
            vm((count, tall + 2, half, 4 * chans), bf16),
            vm((count, 2 * chans, tall * half), bf16),
            vm((count, chans, low * half), bf16),
            vm(latents.shape, f32),
            *columns(tall, chans), *columns(low, chans), *columns(low, 2 * chans), *columns(tall, chans),
            *reducer(10, 2 * chans), *reducer(9, chans),
            vm((8, chans), f32), vm((nr, 8, chans), f32), vm((8, chans), f32), vm((nc, 8, chans), f32),
        ]
        dma = pltpu.SemaphoreType.DMA
        many = 4 * nr + 2 * nc
        scratch += [dma((8,)), dma((4,)), dma((64,)), dma((64,)), dma((many,)), dma((many,)),
                    dma((many,)), dma((many,)), dma((nr + nc,)), dma((nr + nc,))]
        hbm = pl.BlockSpec(memory_space=pl.ANY)
        in_vmem = pl.BlockSpec(memory_space=pltpu.VMEM)
        return pl.pallas_call(
            functools.partial(kernel, (nr, nc, factor)),
            out_shape=[
                jax.ShapeDtypeStruct(latents.shape, f32),
                jax.ShapeDtypeStruct(conv_fine.shape, f32),
                jax.ShapeDtypeStruct(conv_coarse.shape, f32),
                jax.ShapeDtypeStruct(lift.shape, f32),
                jax.ShapeDtypeStruct(time_table.shape, f32),
            ],
            in_specs=[pl.BlockSpec(memory_space=pltpu.SMEM)] + [hbm] * 6,
            out_specs=[hbm] + [in_vmem] * 4,
            scratch_shapes=scratch,
            compiler_params=pltpu.CompilerParams(
                collective_id=0, has_side_effects=True, vmem_limit_bytes=60 * 2**20),
        )(timesteps, latents, cotangent, time_table, conv_fine, conv_coarse, lift)

    in_specs = (P(None, "row", "col", None), P(), P(), P(), P(), P(), P(None, "row", "col", None))
    out_specs = (P(None, "row", "col", None), P(), P(), P(), P())
    return jax.shard_map(body, mesh=mesh, in_specs=in_specs, out_specs=out_specs, check_vma=False)
```

time: 331 us -> 87.5 us (0.26); the launches traced: 326 us -> 87.3 us
  waiting for transfers between devices: 133 us -> 0 us
  matrix products: 95.3 us -> 0 us
  Pallas kernels: 0 us -> 78.5 us
  starting transfers between devices: 49.2 us -> 0 us
  other arithmetic: 22.6 us -> 0 us
  between operations: 14.9 us -> 0.66 us
    psum x1 -> x0, waiting for transfers between devices: 118 us -> none  [body(): lax.psum((lift_part, coarse_part, fine_part, table_part), ('row', 'col'))]
    dot_general x58 -> x0, matrix products: 95.3 us -> none  [the longest x18 40.6 us: forward_taps(): jnp.einsum('bhwc,cd->bhwd', window, kernel[row_tap, col_tap], preferred_e...]
    pallas_call x0 -> x1, Pallas kernels: none -> 78.5 us  [body(): pl.pallas_call(functools.partial(kernel, (nr, nc, factor)), out_shape=[ja...]
    ppermute x16 -> x0, starting transfers between devices: 49.2 us -> none  [the longest x8 35.4 us: extended(): before = lax.ppermute(last, axis, up)]
    ppermute x16 -> x0, waiting for transfers between devices: 15.3 us -> none  [the longest x8 15.3 us: extended(): after = lax.ppermute(first, axis, down)]
    reduce_sum x3 -> x0, other arithmetic: 14.4 us -> none  [the longest x2 9.76 us: block_sum(): return field_in.astype(jnp.float32).reshape(count, tall // 2, 2, broad //...]
    mul x4 -> x0, other arithmetic: 4.86 us -> none  [the longest x1 2.51 us: body(): factor * coarse_total]
    unnamed x47 -> x13, local copies, waits for them, and re-layouts: 4.18 us -> 8.2 us
  transfers between devices with their start and end apart: 17 -> 0, of which waited for: 7 -> 0; matrix products, arithmetic and copies ran while one was open for 19% -> 0% of each run, Pallas kernels for 0% -> 0%
where the time goes in v1:
time: 87.5 us; the launch traced here: 87.3 us
  Pallas kernels  78.5 us (90%)
  local copies, waits for them, and re-layouts  8.2 us (9%)
    pallas_call x1, Pallas kernels, body(): pl.pallas_call(functools.partial(kernel, (nr, nc, factor)), out_shape=[ja...  78.5 us
    unnamed x13, local copies, waits for them, and re-layouts  8.2 us

profile of v1, /device:TPU:1, one launch (start us, length us, event | category | flops | bytes accessed | tf_op | source)
XLA Modules:
  0.0 87.3 jit_solution(14589575550851869458)
XLA Ops:
  0.6 78.5 %shard_map.110 = (f32[2,64,64,128]{3,2,1,0:T(8,128)}, f32[3,3,128,128]{3,2,1,0:T(8,128)}, f32[3,3,128,256]{3,2,1,0:T(8,128)}, f32[256,128]{1,0:T(8,128)}, f32[1000,128]{1,0:T(8,128)}) custom-call(s32[2]{0:T(128)} %times.1, bf16[2,64,64,128]{3,2,1,0:T(8,128)(2,1)} %lat_in.1, bf16[2,64,64,128]{3,2,1,0:T(8,128)(2,1)} %cot_in.1, f32[1000,128]{1,0:T(8,128)} %table_in.1, ...), custom_call_target="tpu_custom_call" | custom-call | tf_op jit(solution)/shard_map/pallas_call | solution.py:562
  79.1 0.0 copy-start.1
  79.1 0.0 copy-start
  79.1 4.9 %copy.17 = f32[2,64,64,128]{3,2,1,0:T(8,128)} copy(f32[2,64,64,128]{3,2,1,0:T(8,128)} %get-tuple-element.10) | data formatting | bytes 8388608
  84.1 0.0 copy-done.1
  84.1 0.0 copy-start.3
  84.1 0.0 copy-start.2
  84.1 0.8 copy.18
  84.9 0.0 copy-done
  84.9 1.0 %copy.19 = f32[3,3,128,256]{3,2,1,0:T(8,128)} copy(f32[3,3,128,256]{3,2,1,0:T(8,128)S(1)} %copy-done) | data formatting | bytes 2359296
  85.9 0.0 copy-done.3
  85.9 0.7 copy.20
  86.6 0.0 copy-done.2
  86.6 0.8 copy.21
Async XLA Ops:
  79.1 4.9 %copy-start.1 = (f32[3,3,128,128]{3,2,1,0:T(8,128)S(1)}, f32[3,3,128,128]{3,2,1,0:T(8,128)}, u32[]{:S(2)}) copy-start(f32[3,3,128,128]{3,2,1,0:T(8,128)} %get-tuple-element.11) | copy-start | bytes 1769476
  79.1 5.8 %copy-start = (f32[3,3,128,256]{3,2,1,0:T(8,128)S(1)}, f32[3,3,128,256]{3,2,1,0:T(8,128)}, u32[]{:S(2)}) copy-start(f32[3,3,128,256]{3,2,1,0:T(8,128)} %get-tuple-element.12) | copy-start | bytes 3538948
  84.1 1.8 %copy-start.3 = (f32[256,128]{1,0:T(8,128)S(1)}, f32[256,128]{1,0:T(8,128)}, u32[]{:S(2)}) copy-start(f32[256,128]{1,0:T(8,128)} %get-tuple-element.13) | copy-start | bytes 393220
  84.1 2.5 %copy-start.2 = (f32[1000,128]{1,0:T(8,128)S(1)}, f32[1000,128]{1,0:T(8,128)}, u32[]{:S(2)}) copy-start(f32[1000,128]{1,0:T(8,128)} %get-tuple-element.14) | copy-start | bytes 1536004

commit v2 on v1

v2 whole, which is shorter than its diff:
```python
import functools
import math

import jax
import jax.numpy as jnp
from jax import lax
from jax.experimental import pallas as pl
from jax.experimental.pallas import tpu as pltpu
from jax.sharding import PartitionSpec as P

MESH = pl.DeviceIdType.MESH
f32 = jnp.float32
bf16 = jnp.bfloat16


def dot(a, b):
    return jnp.dot(a, b, preferred_element_type=f32)


def outer(a, b):
    return lax.dot_general(a, b, (((0,), (0,)), ((), ())), preferred_element_type=f32)


def sigmoid(v):
    return 0.5 + 0.5 * jnp.tanh(0.5 * v)


def shifted(v, column, step):
    n = v.shape[1]
    ids = lax.broadcasted_iota(jnp.int32, v.shape, 1)
    edge = 0 if step == 1 else n - 1
    return jnp.where(ids == edge, column[:, None, :], pltpu.roll(v, step % n, 1))


def kernel(
    sizes,
    times, lat_in, cot_in, table_in, fine_in, coarse_in, lift_in,
    grad_out, a_out, b_out, l_out,
    lat, cot, table, kfine, kcoarse, lift,
    w_fwd, w_back, wc_back, lift_hi, lift_lo,
    V, C2, SL, PO, UG, CB, ACT, GC, G, OUT,
    sc_v, rc_v, sc_p, rc_p, sc_c, rc_c, sc_g, rc_g,
    a_theirs, a_mixed, a_send, a_r1, a_s2, a_r2, a_t, a_f,
    b_send, b_r1, b_s2, b_r2, b_t, b_f,
    l_send, l_r1, l_s2, l_r2, l_f,
    in_sem, out_sem, h_ssem, h_rsem, a_ssem, a_rsem, b_ssem, b_rsem, l_ssem, l_rsem,
):
    nr, nc = sizes
    pairs = nc // 2
    row, col = lax.axis_index("row"), lax.axis_index("col")
    core, pair = lax.rem(col, 2), col // 2
    twin = col + 1 - 2 * core
    up, down = lax.rem(row + nr - 1, nr), lax.rem(row + 1, nr)
    left, right = lax.rem(col + nc - 1, nc), lax.rem(col + 1, nc)
    other = jnp.where(core == 0, left, right)
    count, tall, half = C2.shape[0], C2.shape[1], C2.shape[2]
    low = tall // 2
    chans = lat.shape[3]

    barrier = pltpu.get_barrier_semaphore()
    partners = [(lax.rem(row + d, nr), col) for d in range(1, nr)]
    partners += [(lax.rem(row + d, nr), twin) for d in range(nr)]
    partners += [(row, lax.rem(pair + d, pairs) * 2 + core) for d in range(1, pairs)]
    partners += [(up, other), (row, other), (down, other)]
    for who in partners:
        pl.semaphore_signal(barrier, inc=1, device_id=who, device_id_type=MESH)

    loads = {}

    def load(name, src, dst):
        loads[name] = pltpu.make_async_copy(src, dst, in_sem.at[len(loads)])
        loads[name].start()

    load("lat0", lat_in.at[0], lat.at[0])
    load("lat1", lat_in.at[1], lat.at[1])
    load("kfine", fine_in, kfine)

    sending = []

    def remote(src, dst, ssem, rsem, who):
        return pltpu.make_async_remote_copy(
            src_ref=src, dst_ref=dst, send_sem=ssem, recv_sem=rsem, device_id=who, device_id_type=MESH)

    def exchange(kind, b, buf, n, lo, hi, sc, rc):
        first = (kind * count + b) * 8
        first_col, last_col = sc.at[b, 0], sc.at[b, 1]
        to_left, to_right = rc.at[b, 1], rc.at[b, 0]
        lanes = pl.ds(lo, hi - lo)
        plan = [
            (first_col.at[pl.ds(0, 8)], to_left.at[pl.ds(n + 8, 8)], (up, left)),
            (last_col.at[pl.ds(0, 8)], to_right.at[pl.ds(n + 8, 8)], (up, right)),
            (first_col.at[pl.ds(n - 8, 8)], to_left.at[pl.ds(0, 8)], (down, left)),
            (last_col.at[pl.ds(n - 8, 8)], to_right.at[pl.ds(0, 8)], (down, right)),
            (first_col, to_left.at[pl.ds(8, n)], (row, left)),
            (last_col, to_right.at[pl.ds(8, n)], (row, right)),
            (buf.at[b, 1, :, lanes], buf.at[b, n + 1, :, lanes], (up, col)),
            (buf.at[b, n, :, lanes], buf.at[b, 0, :, lanes], (down, col)),
        ]
        return [remote(src, dst, h_ssem.at[first + at], h_rsem.at[first + at], who)
                for at, (src, dst, who) in enumerate(plan)]

    def send(copies):
        for c in copies:
            c.start()
            sending.append(c)

    def arrive(copies, b, buf, n, lo, hi, rc):
        for c in copies:
            c.wait_recv()
        nothing = jnp.zeros((buf.shape[2], hi - lo), buf.dtype)

        @pl.when(row == 0)
        def _():
            buf[b, 0, :, lo:hi] = nothing
            rc[b, :, 0:8, :] = jnp.zeros((2, 8, rc.shape[3]), f32)

        @pl.when(row == nr - 1)
        def _():
            buf[b, n + 1, :, lo:hi] = nothing
            rc[b, :, n + 8 : n + 16, :] = jnp.zeros((2, 8, rc.shape[3]), f32)

        @pl.when(col == 0)
        def _():
            rc[b, 0] = jnp.zeros(rc.shape[2:], f32)

        @pl.when(col == nc - 1)
        def _():
            rc[b, 1] = jnp.zeros(rc.shape[2:], f32)

    def widen_fine(buf, b, rc):
        before, after = rc[b, 0, 7 : 7 + tall + 2, :], rc[b, 1, 7 : 7 + tall + 2, :]
        odd = buf[b, :, :, 2 * chans : 3 * chans].astype(f32)
        buf[b, :, :, 0:chans] = shifted(odd, before, 1).astype(bf16)
        even = buf[b, :, :, chans : 2 * chans].astype(f32)
        buf[b, :, :, 3 * chans : 4 * chans] = shifted(even, after, -1).astype(bf16)

    def widen_coarse(buf, b, rc):
        wide_by = rc.shape[3]
        before, after = rc[b, 0, 7 : 7 + low + 2, :], rc[b, 1, 7 : 7 + low + 2, :]
        mid = buf[b, :, :, wide_by : 2 * wide_by].astype(f32)
        buf[b, :, :, 0:wide_by] = shifted(mid, before, 1).astype(bf16)
        buf[b, :, :, 2 * wide_by : 3 * wide_by] = shifted(mid, after, -1).astype(bf16)

    def columns_fine(buf, b, sc):
        sc[b, 0] = buf[b, 1 : tall + 1, 0:16, chans : 2 * chans].astype(f32)[:, 0, :]
        sc[b, 1] = buf[b, 1 : tall + 1, half - 16 : half, 2 * chans : 3 * chans].astype(f32)[:, 15, :]

    def columns_coarse(buf, b, sc):
        wide_by = sc.shape[3]
        lanes = slice(wide_by, 2 * wide_by)
        sc[b, 0] = buf[b, 1 : low + 1, 0:16, lanes].astype(f32)[:, 0, :]
        sc[b, 1] = buf[b, 1 : low + 1, half - 16 : half, lanes].astype(f32)[:, 15, :]

    def split_latents(b):
        V[b, 1 : tall + 1, :, chans : 3 * chans] = lat[b].reshape(tall, half, 2 * chans)

    def split_cotangent(b):
        def one(k, _):
            rows = pl.ds(k * 16, 16)
            both = cot[b, rows].reshape(16, half, 2 * chans)
            C2[b, rows] = both
            total = both.astype(f32).reshape(8, 2, half, 2 * chans).sum(axis=1)
            total = total[:, :, :chans] + total[:, :, chans:]
            upper = total.astype(bf16)
            rest = (total - upper.astype(f32)).astype(bf16)
            UG[b, pl.ds(k * 8, 8)] = jnp.concatenate([upper, rest], -1)
            return 0

        lax.fori_loop(0, tall // 16, one, 0)

    def prepare_forward():
        w_fwd[...] = jnp.zeros(w_fwd.shape, bf16)
        for i in range(3):
            base = i * 4 * chans
            for part in range(2):
                for j in range(3):
                    at = base + (part + j) * chans
                    w_fwd[at : at + chans, part * chans : (part + 1) * chans] = kfine[i, j]

    def prepare_back():
        w_back[...] = jnp.zeros(w_back.shape, bf16)
        for i in range(3):
            for j in range(3):
                turned = kfine[i, j].T
                for part in range(2):
                    at = i * 4 * chans + (part + 2 - j) * chans
                    w_back[at : at + chans, part * chans : (part + 1) * chans] = turned
                at = (i * 3 + 2 - j) * 2 * chans
                wc_back[at : at + 2 * chans, :] = kcoarse[i, j].T

    def prepare_lift():
        turned = lift[...].T
        upper = turned.astype(bf16)
        lift_hi[0:chans, :] = upper
        lift_hi[chans : 2 * chans, :] = upper
        lift_lo[...] = (turned - upper.astype(f32)).astype(bf16)

    def lift_back(b):
        ug = UG[b].reshape(low * half, 2 * chans)
        CB[b] = dot(ug, lift_hi[...]) + dot(ug[:, :chans], lift_lo[...])

    def forward_fine(b):
        embedding = table[pl.ds(times[b], 1), :]
        embedding = jnp.concatenate([embedding, embedding], -1)
        step = 16

        def one(k, _):
            taps = [V[b, pl.ds(k * step + i, step)].reshape(step * half, 4 * chans) for i in range(3)]
            pre = dot(jnp.concatenate(taps, -1), w_fwd[...]) + embedding
            s = sigmoid(pre)
            hidden = pre * s
            SL[b, pl.ds(k * step, step)] = (s + hidden * (1.0 - s)).reshape(step, half, 2 * chans)
            hidden = hidden.astype(bf16).astype(f32).reshape(step // 2, 2, half, 2 * chans).sum(axis=1)
            pooled = 0.25 * (hidden[:, :, :chans] + hidden[:, :, chans:])
            PO[b, pl.ds(k * (step // 2) + 1, step // 2), :, chans : 2 * chans] = pooled.astype(bf16)
            return 0

        lax.fori_loop(0, tall // step, one, 0)

    def forward_coarse(b):
        step = 16

        def one(k, _):
            flat = step * half
            taps = [PO[b, pl.ds(k * step + i, step)].reshape(flat, 3 * chans) for i in range(3)]
            weights = kcoarse[...].reshape(9 * chans, 2 * chans)
            pre = dot(jnp.concatenate(taps, -1), weights)
            s = sigmoid(pre)
            act = pre * s
            here = pl.ds(pl.multiple_of(k * flat, flat), flat)
            ACT[b, here, :] = act.astype(bf16)
            grad = (CB[b, here, :] * (s + act * (1.0 - s))).astype(bf16)
            GC[b, pl.ds(k * step + 1, step), :, 2 * chans : 4 * chans] = grad.reshape(step, half, 2 * chans)
            return 0

        lax.fori_loop(0, low // step, one, 0)

    def backward_coarse(b):
        step = 16

        def one(k, total):
            flat = step * half
            taps = [GC[b, pl.ds(k * step + 2 - i, step)].reshape(flat, 6 * chans) for i in range(3)]
            pooled = 0.25 * dot(jnp.concatenate(taps, -1), wc_back[...])
            pooled = pooled.reshape(step, 1, half, chans)
            pooled = jnp.concatenate([pooled, pooled], -1)
            rows = pl.ds(k * 2 * step, 2 * step)
            direct = C2[b, rows].astype(f32).reshape(step, 2, half, 2 * chans)
            slope = SL[b, rows].reshape(step, 2, half, 2 * chans)
            grad = ((direct + pooled) * slope).astype(bf16)
            G[b, pl.ds(k * 2 * step + 1, 2 * step), :, chans : 3 * chans] = grad.reshape(2 * step, half, 2 * chans)
            return total + grad.astype(f32).reshape(2 * flat // 8, 8, 2 * chans).sum(axis=0)

        total = lax.fori_loop(0, low // step, one, jnp.zeros((8, 2 * chans), f32))
        total = total[:, :chans] + total[:, chans:]
        return total.sum(axis=0, keepdims=True)

    stores = []

    def backward_fine(b, part, parts):
        step = 16

        def one(k, _):
            taps = [G[b, pl.ds(k * step + 2 - i, step)].reshape(step * half, 4 * chans) for i in range(3)]
            grad = dot(jnp.concatenate(taps, -1), w_back[...]).astype(bf16)
            OUT[b, pl.ds(k * step, step)] = grad.reshape(step, 2 * half, chans)
            return 0

        each = tall // step // parts
        lax.fori_loop(part * each, (part + 1) * each, one, 0)
        rows = pl.ds(part * each * step, each * step)
        stores.append(pltpu.make_async_copy(OUT.at[b, rows], grad_out.at[b, rows], out_sem.at[len(stores)]))
        stores[-1].start()

    class Reduce:
        def __init__(self, mine, first, part, second, owned, full, ssem, rsem):
            self.refs = mine, first, part, second, owned, full
            self.ssem, self.rsem = ssem, rsem
            self.share, self.half = chans // nr, mine.shape[0] // 2
            self.base2, self.base3 = 2 * nr, 2 * nr + pairs

        def rows_of(self, peer):
            return pl.ds(pl.multiple_of(peer * self.share, self.share), self.share)

        def chunk(self, ref, owner_core, peer):
            return ref.at[pl.ds(owner_core * self.half, self.half), self.rows_of(peer)]

        def copy1(self, d, to_core):
            mine, first = self.refs[:2]
            peer, flip = lax.rem(row + d, nr), lax.rem(core + to_core, 2)
            return remote(self.chunk(mine, to_core, peer), first.at[2 * d + flip],
                          self.ssem.at[2 * d + flip], self.rsem.at[2 * d + flip], (peer, 2 * pair + to_core))

        def scatter(self, to_core):
            pl.when(core != to_core)(self.copy1(0, to_core).start)
            for d in range(1, nr):
                self.copy1(d, to_core).start()

        def copy2(self, d):
            _, _, part, second = self.refs[:4]
            return remote(part, second.at[pair], self.ssem.at[self.base2 + d], self.rsem.at[self.base2 + d],
                          (row, lax.rem(pair + d, pairs) * 2 + core))

        def cross(self):
            mine, first, part, second = self.refs[:4]
            for at in range(1, 2 * nr):
                remote(part, first.at[at], self.ssem.at[at], self.rsem.at[at], (row, twin)).wait_recv()
            total = mine[pl.ds(core * self.half, self.half), self.rows_of(row), :].astype(f32)
            for at in range(1, 2 * nr):
                total = total + first[at].astype(f32)
            part[...] = total.astype(bf16)
            second[pair] = total.astype(bf16)
            for d in range(1, pairs):
                self.copy2(d).start()

        def copy3(self, d, flip):
            owned, full = self.refs[4:]
            peer = lax.rem(row + d, nr)
            at = self.base3 + 2 * d + flip
            return remote(owned, self.chunk(full, core, row), self.ssem.at[at], self.rsem.at[at],
                          (peer, twin if flip else col))

        def collect(self):
            second, owned, full = self.refs[3:]
            for d in range(1, pairs):
                self.copy2(d).wait_recv()
            total = second[0].astype(f32)
            for at in range(1, pairs):
                total = total + second[at].astype(f32)
            owned[...] = total.astype(bf16)
            full[pl.ds(core * self.half, self.half), self.rows_of(row), :] = total.astype(bf16)

        def gather(self):
            self.collect()
            for at in range(1, 2 * nr):
                self.copy3(at // 2, at % 2).start()

        def finish(self):
            for at in range(1, 2 * nr):
                self.copy3(at // 2, at % 2).wait()
            for at in range(1, 2 * nr):
                remote(self.refs[2], self.refs[1].at[at], self.ssem.at[at], self.rsem.at[at], (row, twin)).wait_send()
            for d in range(1, pairs):
                self.copy2(d).wait_send()

    class ReduceByChip(Reduce):
        def __init__(self, theirs, mixed, *rest):
            super().__init__(*rest)
            self.theirs, self.mixed = theirs, mixed

        def copy0(self):
            give = self.refs[0].at[pl.ds((1 - core) * self.half, self.half)]
            return remote(give, self.theirs, self.ssem.at[0], self.rsem.at[0], (row, twin))

        def copy1(self, d):
            peer = lax.rem(row + d, nr)
            return remote(self.mixed.at[:, self.rows_of(peer)], self.refs[1].at[d],
                          self.ssem.at[d], self.rsem.at[d], (peer, col))

        def scatter(self):
            self.copy0().start()

        def scatter_rows(self):
            self.copy0().wait_recv()
            total = self.refs[0][pl.ds(core * self.half, self.half)].astype(f32) + self.theirs[...].astype(f32)
            self.mixed[...] = total.astype(bf16)
            for d in range(1, nr):
                self.copy1(d).start()

        def cross(self):
            _, first, part, second = self.refs[:4]
            for d in range(1, nr):
                self.copy1(d).wait_recv()
            total = self.mixed[:, self.rows_of(row), :].astype(f32)
            for d in range(1, nr):
                total = total + first[d].astype(f32)
            part[...] = total.astype(bf16)
            second[pair] = total.astype(bf16)
            for d in range(1, pairs):
                self.copy2(d).start()

        def gather(self):
            self.collect()
            for d in range(1, nr):
                self.copy3(d, 0).start()

        def copy4(self):
            done = self.refs[5].at[pl.ds(core * self.half, self.half)]
            return remote(done, done, self.ssem.at[nr], self.rsem.at[nr], (row, twin))

        def gather_cores(self):
            for d in range(1, nr):
                self.copy3(d, 0).wait_recv()
            self.copy4().start()

        def finish(self):
            self.copy4().wait()
            self.copy0().wait_send()
            for d in range(1, nr):
                self.copy1(d).wait_send()
                self.copy3(d, 0).wait_send()
            for d in range(1, pairs):
                self.copy2(d).wait_send()

    sum_a = ReduceByChip(a_theirs, a_mixed, a_send, a_r1, a_s2, a_r2, a_t, a_f, a_ssem, a_rsem)
    sum_b = Reduce(b_send, b_r1, b_s2, b_r2, b_t, b_f, b_ssem, b_rsem)

    ex_v = [(b, V, tall, chans, 3 * chans) for b in range(count)]
    ex_p = [(b, PO, low, chans, 2 * chans) for b in range(count)]
    ex_c = [(b, GC, low, 2 * chans, 4 * chans) for b in range(count)]
    ex_g = [(b, G, tall, chans, 3 * chans) for b in range(count)]
    loads["lat0"].wait()
    split_latents(0)
    columns_fine(V, 0, sc_v)
    pl.semaphore_wait(barrier, len(partners))
    moving_v = [exchange(0, *ex_v[b], sc_v, rc_v) for b in range(count)]
    send(moving_v[0])
    loads["lat1"].wait()
    split_latents(1)
    columns_fine(V, 1, sc_v)
    send(moving_v[1])
    load("table", table_in, table)
    load("cot0", cot_in.at[0], cot.at[0])
    load("cot1", cot_in.at[1], cot.at[1])
    load("lift", lift_in, lift)
    load("kcoarse", coarse_in, kcoarse)
    loads["kfine"].wait()
    prepare_forward()
    loads["cot0"].wait()
    split_cotangent(0)
    loads["cot1"].wait()
    split_cotangent(1)
    loads["table"].wait()
    loads["kcoarse"].wait()

    moving_p = [exchange(1, *ex_p[b], sc_p, rc_p) for b in range(count)]
    for b in range(count):
        arrive(moving_v[b], *ex_v[b], rc_v)
        widen_fine(V, b, rc_v)
        forward_fine(b)
        columns_coarse(PO, b, sc_p)
        send(moving_p[b])

    loads["lift"].wait()
    prepare_lift()
    lift_back(0)
    lift_back(1)
    prepare_back()

    moving_c = [exchange(2, *ex_c[b], sc_c, rc_c) for b in range(count)]
    for b in range(count):
        arrive(moving_p[b], *ex_p[b], rc_p)
        widen_coarse(PO, b, rc_p)
        forward_coarse(b)
        columns_coarse(GC, b, sc_c)
        send(moving_c[b])

    lifted = jnp.zeros((2 * chans, 2 * chans), f32)
    for b in range(count):
        lifted = lifted + outer(ACT[b], UG[b].reshape(low * half, 2 * chans))
    lifted = (lifted[:, :chans] + lifted[:, chans:]).astype(bf16)
    a_send[9, :, 0:chans] = lifted[:chans]
    a_send[9, :, chans : 2 * chans] = lifted[chans:]
    for i in range(3):
        kernel_grad = jnp.zeros((2 * chans, 3 * chans), f32)
        for b in range(count):
            grad = GC[b, 1 : low + 1, :, 2 * chans : 4 * chans].reshape(low * half, 2 * chans)
            kernel_grad = kernel_grad + outer(grad, PO[b, i : i + low].reshape(low * half, 3 * chans))
        for j in range(3):
            a_send[3 * i + j] = kernel_grad[:, j * chans : (j + 1) * chans].T.astype(bf16)
    sum_a.scatter()

    moving_g = [exchange(3, *ex_g[b], sc_g, rc_g) for b in range(count)]
    sums = []
    for b in range(count):
        arrive(moving_c[b], *ex_c[b], rc_c)
        widen_coarse(GC, b, rc_c)
        sums.append(backward_coarse(b))
        columns_fine(G, b, sc_g)
        send(moving_g[b])
        if b == 0:
            sum_a.scatter_rows()

    l_send[...] = jnp.concatenate(sums + [jnp.zeros((8 - count, chans), f32)], 0)
    l_moving = [
        remote(l_send, l_r1.at[2 * row + core], l_ssem.at[at], l_rsem.at[at],
               (lax.rem(row + at // 2, nr), twin if at % 2 else col))
        for at in range(1, 2 * nr)
    ]
    send(l_moving)
    l_r1[2 * row + core] = l_send[...]

    for i in range(3):
        kernel_grad = jnp.zeros((2 * chans, 4 * chans), f32)
        for b in range(count):
            grad = G[b, 1 : tall + 1, :, chans : 3 * chans].reshape(tall * half, 2 * chans)
            kernel_grad = kernel_grad + outer(grad, V[b, i : i + tall].reshape(tall * half, 4 * chans))
        for j in range(3):
            both = kernel_grad[:chans, j * chans : (j + 1) * chans]
            both = both + kernel_grad[chans:, (j + 1) * chans : (j + 2) * chans]
            b_send[3 * i + j] = both.astype(bf16)
        if i == 1:
            sum_b.scatter(0)
    b_send[9] = jnp.zeros(b_send.shape[1:], bf16)
    sum_b.scatter(1)

    arrive(moving_g[0], *ex_g[0], rc_g)
    widen_fine(G, 0, rc_g)
    sum_a.cross()
    backward_fine(0, 0, 2)
    backward_fine(0, 1, 2)
    for c in l_moving:
        c.wait_recv()
    total = l_r1[0]
    for at in range(1, 2 * nr):
        total = total + l_r1[at]
    l_s2[...] = total
    l_r2[pair] = total
    l_moving2 = [
        remote(l_s2, l_r2.at[pair], l_ssem.at[2 * nr + d], l_rsem.at[2 * nr + d],
               (row, lax.rem(pair + d, pairs) * 2 + core))
        for d in range(1, pairs)
    ]
    send(l_moving2)

    arrive(moving_g[1], *ex_g[1], rc_g)
    widen_fine(G, 1, rc_g)
    backward_fine(1, 0, 2)
    sum_b.cross()
    backward_fine(1, 1, 2)
    sum_a.gather()
    sum_b.gather()
    sum_a.gather_cores()

    for c in l_moving2:
        c.wait_recv()
    total = l_r2[0]
    for d in range(1, pairs):
        total = total + l_r2[d]
    l_send_done = pltpu.make_async_copy(l_f, l_out, out_sem.at[len(stores)])
    l_f[...] = total
    l_send_done.start()
    stores.append(l_send_done)
    sum_a.finish()
    stores.append(pltpu.make_async_copy(a_f, a_out, out_sem.at[len(stores)]))
    stores[-1].start()
    for c in sending:
        c.wait_send()
    sum_b.finish()
    stores.append(pltpu.make_async_copy(b_f, b_out, out_sem.at[len(stores)]))
    stores[-1].start()
    for c in stores:
        c.wait()


def finishing(
    factor, parts, times, grad_in, a_in, b_in, l_in, grad_out, fine_out, coarse_out, lift_out, table_out,
    g16, a16, b16, l32, g32, fine, coarse, lift, table, in_sem, out_sem,
):
    count, tall, chans = g16.shape[0], g16.shape[1], g16.shape[3]
    each = tall // parts
    pieces = [(b, pl.ds(p * each, each)) for b in range(count) for p in range(parts)]
    loads = [pltpu.make_async_copy(grad_in.at[b, rows], g16.at[b, rows], in_sem.at[3 + at])
             for at, (b, rows) in enumerate(pieces)]
    loads += [pltpu.make_async_copy(l_in, l32, in_sem.at[0]), pltpu.make_async_copy(b_in, b16, in_sem.at[1]),
              pltpu.make_async_copy(a_in, a16, in_sem.at[2])]
    for c in loads:
        c.start()
    stores = []

    def store(src, dst):
        stores.append(pltpu.make_async_copy(src, dst, out_sem.at[len(stores)]))
        stores[-1].start()

    for at, (b, rows) in enumerate(pieces):
        loads[at].wait()
        g32[b, rows] = g16[b, rows].astype(f32)
        store(g32.at[b, rows], grad_out.at[b, rows])
    loads[-3].wait()
    total = factor * l32[...]
    ids = lax.broadcasted_iota(jnp.int32, table.shape, 0)
    placed = jnp.zeros(table.shape, f32)
    for b in range(count):
        placed = placed + jnp.where(ids == times[b], total[b : b + 1, :], 0.0)
    table[...] = placed
    store(table, table_out)
    loads[-2].wait()
    for t in range(9):
        fine[t // 3, t % 3] = factor * b16[t].astype(f32).T
    store(fine, fine_out)
    loads[-1].wait()
    for t in range(9):
        coarse[t // 3, t % 3] = factor * a16[t].astype(f32)
    store(coarse, coarse_out)
    lift[0:chans, :] = factor * a16[9, :, 0:chans].astype(f32)
    lift[chans : 2 * chans, :] = factor * a16[9, :, chans : 2 * chans].astype(f32)
    store(lift, lift_out)
    for c in stores:
        c.wait()


def solution(mesh):
    nr, nc = mesh.shape["row"], mesh.shape["col"]

    def body(latents, timesteps, time_table, conv_fine, conv_coarse, lift, cotangent):
        count, tall, broad, chans = latents.shape
        half, low = broad // 2, tall // 2
        share, pairs = chans // nr, nc // 2
        factor = 1.0 / math.sqrt(count * tall * broad * nr * nc)
        vm = pltpu.VMEM
        dma = pltpu.SemaphoreType.DMA
        hbm = pl.BlockSpec(memory_space=pl.ANY)
        smem = pl.BlockSpec(memory_space=pltpu.SMEM)

        def reducer(wide, peers):
            return [
                vm((10, chans, wide), bf16),
                vm((peers, 5, share, wide), bf16),
                vm((5, share, wide), bf16),
                vm((pairs, 5, share, wide), bf16),
                vm((5, share, wide), bf16),
                vm((10, chans, wide), bf16),
            ]

        def columns(n, wide):
            return [vm((count, 2, n, wide), f32), vm((count, 2, n + 16, wide), f32)]

        scratch = [
            vm(latents.shape, bf16), vm(cotangent.shape, bf16), vm(time_table.shape, f32),
            vm(conv_fine.shape, bf16), vm(conv_coarse.shape, bf16), vm(lift.shape, f32),
            vm((12 * chans, 2 * chans), bf16), vm((12 * chans, 2 * chans), bf16), vm((18 * chans, chans), bf16),
            vm((2 * chans, 2 * chans), bf16), vm((chans, 2 * chans), bf16),
            vm((count, tall + 2, half, 4 * chans), bf16),
            vm((count, tall, half, 2 * chans), bf16),
            vm((count, tall, half, 2 * chans), f32),
            vm((count, low + 2, half, 3 * chans), bf16),
            vm((count, low, half, 2 * chans), bf16),
            vm((count, low * half, 2 * chans), f32),
            vm((count, low * half, 2 * chans), bf16),
            vm((count, low + 2, half, 6 * chans), bf16),
            vm((count, tall + 2, half, 4 * chans), bf16),
            vm(latents.shape, bf16),
            *columns(tall, chans), *columns(low, chans), *columns(low, 2 * chans), *columns(tall, chans),
            vm((5, chans, 2 * chans), bf16), vm((5, chans, 2 * chans), bf16), *reducer(2 * chans, nr), *reducer(chans, 2 * nr),
            vm((8, chans), f32), vm((2 * nr, 8, chans), f32), vm((8, chans), f32), vm((pairs, 8, chans), f32),
            vm((8, chans), f32),
        ]
        many = 4 * nr + pairs
        scratch += [dma((8,)), dma((8,)), dma((64,)), dma((64,)), dma((many,)), dma((many,)),
                    dma((many,)), dma((many,)), dma((2 * nr + pairs,)), dma((2 * nr + pairs,))]
        shape = jax.ShapeDtypeStruct
        grad, sum_a, sum_b, sum_l = pl.pallas_call(
            functools.partial(kernel, (nr, nc)),
            out_shape=[shape(latents.shape, bf16), shape((10, chans, 2 * chans), bf16),
                       shape((10, chans, chans), bf16), shape((8, chans), f32)],
            in_specs=[smem] + [hbm] * 6,
            out_specs=[hbm] * 4,
            scratch_shapes=scratch,
            compiler_params=pltpu.CompilerParams(
                collective_id=0, has_side_effects=True, vmem_limit_bytes=60 * 2**20),
        )(timesteps, latents, cotangent, time_table, conv_fine, conv_coarse, lift)

        parts = 4
        results = [latents.shape, conv_fine.shape, conv_coarse.shape, lift.shape, time_table.shape]
        return pl.pallas_call(
            functools.partial(finishing, factor, parts),
            out_shape=[shape(s, f32) for s in results],
            in_specs=[smem] + [hbm] * 4,
            out_specs=[hbm] * 5,
            scratch_shapes=[
                vm(latents.shape, bf16), vm(sum_a.shape, bf16), vm(sum_b.shape, bf16), vm(sum_l.shape, f32),
                *[vm(s, f32) for s in results], dma((3 + count * parts,)), dma((4 + count * parts,))],
            compiler_params=pltpu.CompilerParams(vmem_limit_bytes=60 * 2**20),
        )(timesteps, grad, sum_a, sum_b, sum_l)

    in_specs = (P(None, "row", "col", None), P(), P(), P(), P(), P(), P(None, "row", "col", None))
    out_specs = (P(None, "row", "col", None), P(), P(), P(), P())
    return jax.shard_map(body, mesh=mesh, in_specs=in_specs, out_specs=out_specs, check_vma=False)
```

time: 87.5 us -> 66.1 us (0.76)
  Pallas kernels: 78.5 us -> 65 us
  local copies, waits for them, and re-layouts: 8.2 us -> 0 us
    pallas_call x1 -> x2, Pallas kernels: 78.5 us -> 65 us  [the longest x1 60.5 us: body(): pl.pallas_call(functools.partial(kernel, (nr, nc)), out_shape=[shape(late...]
    unnamed x13 -> x0, local copies, waits for them, and re-layouts: 8.2 us -> none
where the time goes in v2:
time: 66.1 us; the launch traced here: 65.9 us
  Pallas kernels  65 us (98%)
  between operations  0.8 us (1%)
    pallas_call x1, Pallas kernels, body(): pl.pallas_call(functools.partial(kernel, (nr, nc)), out_shape=[shape(late...  60.5 us
    pallas_call x1, Pallas kernels, body(): pl.pallas_call(functools.partial(finishing, factor, parts), out_shape=[sh...  4.58 us

profile of v2, /device:TPU:1, one launch (start us, length us, event | category | flops | bytes accessed | tf_op | source)
XLA Modules:
  0.0 65.9 jit_solution(3289833137703531813)
XLA Ops:
  0.6 60.5 %shard_map.110 = (bf16[2,64,64,128]{3,2,1,0:T(8,128)(2,1)}, bf16[10,128,256]{2,1,0:T(8,128)(2,1)}, bf16[10,128,128]{2,1,0:T(8,128)(2,1)}, f32[8,128]{1,0:T(8,128)}) custom-call(s32[2]{0:T(128)} %times.3, bf16[2,64,64,128]{3,2,1,0:T(8,128)(2,1)} %lat_in.1, bf16[2,64,64,128]{3,2,1,0:T(8,128)(2,1)} %cot_in.1, f32[1000,128]{1,0:T(8,128)} %table_in.1, ...), custom_call_target="tpu_custom_call" | custom-call | tf_op jit(solution)/shard_map/pallas_call | solution.py:652
  61.1 4.6 %shard_map.111 = (f32[2,64,64,128]{3,2,1,0:T(8,128)}, f32[3,3,128,128]{3,2,1,0:T(8,128)}, f32[3,3,128,256]{3,2,1,0:T(8,128)}, f32[256,128]{1,0:T(8,128)}, f32[1000,128]{1,0:T(8,128)}) custom-call(s32[2]{0:T(128)} %times.3, bf16[2,64,64,128]{3,2,1,0:T(8,128)(2,1)} %get-tuple-element.9.grad_in, bf16[10,128,256]{2,1,0:T(8,128)(2,1)} %get-tuple-element.10.a_in, ...), custom_call_target="tpu_custom_call" | custom-call | tf_op jit(solution)/shard_map/pallas_call | solution.py:665

commit v3 on v2

--- a/solution.py
+++ b/solution.py
@@ -34,9 +34,9 @@
 
 def kernel(
     sizes,
-    times, lat_in, cot_in, table_in, fine_in, coarse_in, lift_in,
+    times_in, lat_in, cot_in, table_in, fine_in, coarse_in, lift_in,
     grad_out, a_out, b_out, l_out,
-    lat, cot, table, kfine, kcoarse, lift,
+    times, lat, cot, table, kfine, kcoarse, lift,
     w_fwd, w_back, wc_back, lift_hi, lift_lo,
     V, C2, SL, PO, UG, CB, ACT, GC, G, OUT,
     sc_v, rc_v, sc_p, rc_p, sc_c, rc_c, sc_g, rc_g,
@@ -74,6 +74,7 @@
     load("lat0", lat_in.at[0], lat.at[0])
     load("lat1", lat_in.at[1], lat.at[1])
     load("kfine", fine_in, kfine)
+    load("times", times_in, times)
 
     sending = []
 
@@ -82,7 +83,7 @@
             src_ref=src, dst_ref=dst, send_sem=ssem, recv_sem=rsem, device_id=who, device_id_type=MESH)
 
     def exchange(kind, b, buf, n, lo, hi, sc, rc):
-        first = (kind * count + b) * 8
+        at = kind * count + b
         first_col, last_col = sc.at[b, 0], sc.at[b, 1]
         to_left, to_right = rc.at[b, 1], rc.at[b, 0]
         lanes = pl.ds(lo, hi - lo)
@@ -96,17 +97,18 @@
             (buf.at[b, 1, :, lanes], buf.at[b, n + 1, :, lanes], (up, col)),
             (buf.at[b, n, :, lanes], buf.at[b, 0, :, lanes], (down, col)),
         ]
-        return [remote(src, dst, h_ssem.at[first + at], h_rsem.at[first + at], who)
-                for at, (src, dst, who) in enumerate(plan)]
+        rows = sum(math.prod(src.shape) * jnp.dtype(src.dtype).itemsize for src, _, _ in plan) // (4 * chans)
+        every = table.at[pl.ds(0, rows)]
+        return ([remote(src, dst, h_ssem.at[at], h_rsem.at[at], who) for src, dst, who in plan],
+                remote(every, every, h_ssem.at[at], h_rsem.at[at], (row, twin)))
 
     def send(copies):
-        for c in copies:
+        for c in copies[0]:
             c.start()
-            sending.append(c)
+        sending.append(copies[1])
 
     def arrive(copies, b, buf, n, lo, hi, rc):
-        for c in copies:
-            c.wait_recv()
+        copies[1].wait_recv()
         nothing = jnp.zeros((buf.shape[2], hi - lo), buf.dtype)
 
         @pl.when(row == 0)
@@ -202,7 +204,7 @@
     def forward_fine(b):
         embedding = table[pl.ds(times[b], 1), :]
         embedding = jnp.concatenate([embedding, embedding], -1)
-        step = 16
+        step = 32
 
         def one(k, _):
             taps = [V[b, pl.ds(k * step + i, step)].reshape(step * half, 4 * chans) for i in range(3)]
@@ -218,7 +220,7 @@
         lax.fori_loop(0, tall // step, one, 0)
 
     def forward_coarse(b):
-        step = 16
+        step = 32
 
         def one(k, _):
             flat = step * half
@@ -236,7 +238,7 @@
         lax.fori_loop(0, low // step, one, 0)
 
     def backward_coarse(b):
-        step = 16
+        step = 32
 
         def one(k, total):
             flat = step * half
@@ -258,7 +260,7 @@
     stores = []
 
     def backward_fine(b, part, parts):
-        step = 16
+        step = 32
 
         def one(k, _):
             taps = [G[b, pl.ds(k * step + 2 - i, step)].reshape(step * half, 4 * chans) for i in range(3)]
@@ -277,7 +279,11 @@
             self.refs = mine, first, part, second, owned, full
             self.ssem, self.rsem = ssem, rsem
             self.share, self.half = chans // nr, mine.shape[0] // 2
-            self.base2, self.base3 = 2 * nr, 2 * nr + pairs
+            self.peers = first.shape[0] - 1
+
+        def all_of(self, phase):
+            every = self.refs[3].at[pl.ds(0, pairs - 1)] if phase == 2 else self.refs[1].at[pl.ds(1, self.peers)]
+            return remote(every, every, self.ssem.at[phase], self.rsem.at[phase], (row, twin))
 
         def rows_of(self, peer):
             return pl.ds(pl.multiple_of(peer * self.share, self.share), self.share)
@@ -289,7 +295,7 @@
             mine, first = self.refs[:2]
             peer, flip = lax.rem(row + d, nr), lax.rem(core + to_core, 2)
             return remote(self.chunk(mine, to_core, peer), first.at[2 * d + flip],
-                          self.ssem.at[2 * d + flip], self.rsem.at[2 * d + flip], (peer, 2 * pair + to_core))
+                          self.ssem.at[1], self.rsem.at[1], (peer, 2 * pair + to_core))
 
         def scatter(self, to_core):
             pl.when(core != to_core)(self.copy1(0, to_core).start)
@@ -298,13 +304,12 @@
 
         def copy2(self, d):
             _, _, part, second = self.refs[:4]
-            return remote(part, second.at[pair], self.ssem.at[self.base2 + d], self.rsem.at[self.base2 + d],
+            return remote(part, second.at[pair], self.ssem.at[2], self.rsem.at[2],
                           (row, lax.rem(pair + d, pairs) * 2 + core))
 
         def cross(self):
             mine, first, part, second = self.refs[:4]
-            for at in range(1, 2 * nr):
-                remote(part, first.at[at], self.ssem.at[at], self.rsem.at[at], (row, twin)).wait_recv()
+            self.all_of(1).wait_recv()
             total = mine[pl.ds(core * self.half, self.half), self.rows_of(row), :].astype(f32)
             for at in range(1, 2 * nr):
                 total = total + first[at].astype(f32)
@@ -316,14 +321,12 @@
         def copy3(self, d, flip):
             owned, full = self.refs[4:]
             peer = lax.rem(row + d, nr)
-            at = self.base3 + 2 * d + flip
-            return remote(owned, self.chunk(full, core, row), self.ssem.at[at], self.rsem.at[at],
+            return remote(owned, self.chunk(full, core, row), self.ssem.at[3], self.rsem.at[3],
                           (peer, twin if flip else col))
 
         def collect(self):
             second, owned, full = self.refs[3:]
-            for d in range(1, pairs):
-                self.copy2(d).wait_recv()
+            self.all_of(2).wait_recv()
             total = second[0].astype(f32)
             for at in range(1, pairs):
                 total = total + second[at].astype(f32)
@@ -336,12 +339,9 @@
                 self.copy3(at // 2, at % 2).start()
 
         def finish(self):
-            for at in range(1, 2 * nr):
-                self.copy3(at // 2, at % 2).wait()
-            for at in range(1, 2 * nr):
-                remote(self.refs[2], self.refs[1].at[at], self.ssem.at[at], self.rsem.at[at], (row, twin)).wait_send()
-            for d in range(1, pairs):
-                self.copy2(d).wait_send()
+            self.all_of(3).wait_recv()
+            for phase in range(1, 4):
+                self.all_of(phase).wait_send()
 
     class ReduceByChip(Reduce):
         def __init__(self, theirs, mixed, *rest):
@@ -355,22 +355,21 @@
         def copy1(self, d):
             peer = lax.rem(row + d, nr)
             return remote(self.mixed.at[:, self.rows_of(peer)], self.refs[1].at[d],
-                          self.ssem.at[d], self.rsem.at[d], (peer, col))
+                          self.ssem.at[1], self.rsem.at[1], (peer, col))
 
         def scatter(self):
             self.copy0().start()
 
         def scatter_rows(self):
             self.copy0().wait_recv()
-            total = self.refs[0][pl.ds(core * self.half, self.half)].astype(f32) + self.theirs[...].astype(f32)
+            total = self.refs[0][pl.ds(core * self.half, self.half)] + self.theirs[...]
             self.mixed[...] = total.astype(bf16)
             for d in range(1, nr):
                 self.copy1(d).start()
 
         def cross(self):
             _, first, part, second = self.refs[:4]
-            for d in range(1, nr):
-                self.copy1(d).wait_recv()
+            self.all_of(1).wait_recv()
             total = self.mixed[:, self.rows_of(row), :].astype(f32)
             for d in range(1, nr):
                 total = total + first[d].astype(f32)
@@ -386,21 +385,17 @@
 
         def copy4(self):
             done = self.refs[5].at[pl.ds(core * self.half, self.half)]
-            return remote(done, done, self.ssem.at[nr], self.rsem.at[nr], (row, twin))
+            return remote(done, done, self.ssem.at[4], self.rsem.at[4], (row, twin))
 
         def gather_cores(self):
-            for d in range(1, nr):
-                self.copy3(d, 0).wait_recv()
+            self.all_of(3).wait_recv()
             self.copy4().start()
 
         def finish(self):
             self.copy4().wait()
             self.copy0().wait_send()
-            for d in range(1, nr):
-                self.copy1(d).wait_send()
-                self.copy3(d, 0).wait_send()
-            for d in range(1, pairs):
-                self.copy2(d).wait_send()
+            for phase in range(1, 4):
+                self.all_of(phase).wait_send()
 
     sum_a = ReduceByChip(a_theirs, a_mixed, a_send, a_r1, a_s2, a_r2, a_t, a_f, a_ssem, a_rsem)
     sum_b = Reduce(b_send, b_r1, b_s2, b_r2, b_t, b_f, b_ssem, b_rsem)
@@ -431,6 +426,7 @@
     loads["cot1"].wait()
     split_cotangent(1)
     loads["table"].wait()
+    loads["times"].wait()
     loads["kcoarse"].wait()
 
     moving_p = [exchange(1, *ex_p[b], sc_p, rc_p) for b in range(count)]
@@ -458,7 +454,7 @@
     lifted = jnp.zeros((2 * chans, 2 * chans), f32)
     for b in range(count):
         lifted = lifted + outer(ACT[b], UG[b].reshape(low * half, 2 * chans))
-    lifted = (lifted[:, :chans] + lifted[:, chans:]).astype(bf16)
+    lifted = lifted[:, :chans] + lifted[:, chans:]
     a_send[9, :, 0:chans] = lifted[:chans]
     a_send[9, :, chans : 2 * chans] = lifted[chans:]
     for i in range(3):
@@ -467,7 +463,7 @@
             grad = GC[b, 1 : low + 1, :, 2 * chans : 4 * chans].reshape(low * half, 2 * chans)
             kernel_grad = kernel_grad + outer(grad, PO[b, i : i + low].reshape(low * half, 3 * chans))
         for j in range(3):
-            a_send[3 * i + j] = kernel_grad[:, j * chans : (j + 1) * chans].T.astype(bf16)
+            a_send[3 * i + j] = kernel_grad[:, j * chans : (j + 1) * chans].T
     sum_a.scatter()
 
     moving_g = [exchange(3, *ex_g[b], sc_g, rc_g) for b in range(count)]
@@ -483,10 +479,12 @@
 
     l_send[...] = jnp.concatenate(sums + [jnp.zeros((8 - count, chans), f32)], 0)
     l_moving = [
-        remote(l_send, l_r1.at[2 * row + core], l_ssem.at[at], l_rsem.at[at],
+        remote(l_send, l_r1.at[2 * row + core], l_ssem.at[0], l_rsem.at[0],
                (lax.rem(row + at // 2, nr), twin if at % 2 else col))
         for at in range(1, 2 * nr)
     ]
+    every = l_r1.at[pl.ds(0, 2 * nr - 1)]
+    l_moving = l_moving, remote(every, every, l_ssem.at[0], l_rsem.at[0], (row, twin))
     send(l_moving)
     l_r1[2 * row + core] = l_send[...]
 
@@ -509,18 +507,19 @@
     sum_a.cross()
     backward_fine(0, 0, 2)
     backward_fine(0, 1, 2)
-    for c in l_moving:
-        c.wait_recv()
+    l_moving[1].wait_recv()
     total = l_r1[0]
     for at in range(1, 2 * nr):
         total = total + l_r1[at]
     l_s2[...] = total
     l_r2[pair] = total
     l_moving2 = [
-        remote(l_s2, l_r2.at[pair], l_ssem.at[2 * nr + d], l_rsem.at[2 * nr + d],
+        remote(l_s2, l_r2.at[pair], l_ssem.at[1], l_rsem.at[1],
                (row, lax.rem(pair + d, pairs) * 2 + core))
         for d in range(1, pairs)
     ]
+    every = l_r2.at[pl.ds(0, pairs - 1)]
+    l_moving2 = l_moving2, remote(every, every, l_ssem.at[1], l_rsem.at[1], (row, twin))
     send(l_moving2)
 
     arrive(moving_g[1], *ex_g[1], rc_g)
@@ -532,8 +531,7 @@
     sum_b.gather()
     sum_a.gather_cores()
 
-    for c in l_moving2:
-        c.wait_recv()
+    l_moving2[1].wait_recv()
     total = l_r2[0]
     for d in range(1, pairs):
         total = total + l_r2[d]
@@ -554,15 +552,15 @@
 
 
 def finishing(
-    factor, parts, times, grad_in, a_in, b_in, l_in, grad_out, fine_out, coarse_out, lift_out, table_out,
-    g16, a16, b16, l32, g32, fine, coarse, lift, table, in_sem, out_sem,
+    factor, parts, times_in, grad_in, a_in, b_in, l_in, grad_out, fine_out, coarse_out, lift_out, table_out,
+    times, g16, a16, b16, l32, g32, fine, coarse, lift, table, in_sem, out_sem,
 ):
     count, tall, chans = g16.shape[0], g16.shape[1], g16.shape[3]
     each = tall // parts
     pieces = [(b, pl.ds(p * each, each)) for b in range(count) for p in range(parts)]
-    loads = [pltpu.make_async_copy(grad_in.at[b, rows], g16.at[b, rows], in_sem.at[3 + at])
+    loads = [pltpu.make_async_copy(grad_in.at[b, rows], g16.at[b, rows], in_sem.at[4 + at])
              for at, (b, rows) in enumerate(pieces)]
-    loads += [pltpu.make_async_copy(l_in, l32, in_sem.at[0]), pltpu.make_async_copy(b_in, b16, in_sem.at[1]),
+    loads += [pltpu.make_async_copy(times_in, times, in_sem.at[3]), pltpu.make_async_copy(l_in, l32, in_sem.at[0]), pltpu.make_async_copy(b_in, b16, in_sem.at[1]),
               pltpu.make_async_copy(a_in, a16, in_sem.at[2])]
     for c in loads:
         c.start()
@@ -576,6 +574,7 @@
         loads[at].wait()
         g32[b, rows] = g16[b, rows].astype(f32)
         store(g32.at[b, rows], grad_out.at[b, rows])
+    loads[-4].wait()
     loads[-3].wait()
     total = factor * l32[...]
     ids = lax.broadcasted_iota(jnp.int32, table.shape, 0)
@@ -610,11 +609,10 @@
         vm = pltpu.VMEM
         dma = pltpu.SemaphoreType.DMA
         hbm = pl.BlockSpec(memory_space=pl.ANY)
-        smem = pl.BlockSpec(memory_space=pltpu.SMEM)
-
-        def reducer(wide, peers):
+
+        def reducer(wide, peers, kind):
             return [
-                vm((10, chans, wide), bf16),
+                vm((10, chans, wide), kind),
                 vm((peers, 5, share, wide), bf16),
                 vm((5, share, wide), bf16),
                 vm((pairs, 5, share, wide), bf16),
@@ -626,7 +624,7 @@
             return [vm((count, 2, n, wide), f32), vm((count, 2, n + 16, wide), f32)]
 
         scratch = [
-            vm(latents.shape, bf16), vm(cotangent.shape, bf16), vm(time_table.shape, f32),
+            pltpu.SMEM(timesteps.shape, jnp.int32), vm(latents.shape, bf16), vm(cotangent.shape, bf16), vm(time_table.shape, f32),
             vm(conv_fine.shape, bf16), vm(conv_coarse.shape, bf16), vm(lift.shape, f32),
             vm((12 * chans, 2 * chans), bf16), vm((12 * chans, 2 * chans), bf16), vm((18 * chans, chans), bf16),
             vm((2 * chans, 2 * chans), bf16), vm((chans, 2 * chans), bf16),
@@ -641,19 +639,19 @@
             vm((count, tall + 2, half, 4 * chans), bf16),
             vm(latents.shape, bf16),
             *columns(tall, chans), *columns(low, chans), *columns(low, 2 * chans), *columns(tall, chans),
-            vm((5, chans, 2 * chans), bf16), vm((5, chans, 2 * chans), bf16), *reducer(2 * chans, nr), *reducer(chans, 2 * nr),
+            vm((5, chans, 2 * chans), f32), vm((5, chans, 2 * chans), bf16),
+            *reducer(2 * chans, nr, f32), *reducer(chans, 2 * nr, bf16),
             vm((8, chans), f32), vm((2 * nr, 8, chans), f32), vm((8, chans), f32), vm((pairs, 8, chans), f32),
             vm((8, chans), f32),
         ]
-        many = 4 * nr + pairs
-        scratch += [dma((8,)), dma((8,)), dma((64,)), dma((64,)), dma((many,)), dma((many,)),
-                    dma((many,)), dma((many,)), dma((2 * nr + pairs,)), dma((2 * nr + pairs,))]
+        scratch += [dma((9,)), dma((7,)), dma((4 * count,)), dma((4 * count,)), dma((5,)), dma((5,)),
+                    dma((5,)), dma((5,)), dma((2,)), dma((2,))]
         shape = jax.ShapeDtypeStruct
         grad, sum_a, sum_b, sum_l = pl.pallas_call(
             functools.partial(kernel, (nr, nc)),
             out_shape=[shape(latents.shape, bf16), shape((10, chans, 2 * chans), bf16),
                        shape((10, chans, chans), bf16), shape((8, chans), f32)],
-            in_specs=[smem] + [hbm] * 6,
+            in_specs=[hbm] * 7,
             out_specs=[hbm] * 4,
             scratch_shapes=scratch,
             compiler_params=pltpu.CompilerParams(
@@ -665,11 +663,11 @@
         return pl.pallas_call(
             functools.partial(finishing, factor, parts),
             out_shape=[shape(s, f32) for s in results],
-            in_specs=[smem] + [hbm] * 4,
+            in_specs=[hbm] * 5,
             out_specs=[hbm] * 5,
             scratch_shapes=[
-                vm(latents.shape, bf16), vm(sum_a.shape, bf16), vm(sum_b.shape, bf16), vm(sum_l.shape, f32),
-                *[vm(s, f32) for s in results], dma((3 + count * parts,)), dma((4 + count * parts,))],
+                pltpu.SMEM(timesteps.shape, jnp.int32), vm(latents.shape, bf16), vm(sum_a.shape, bf16), vm(sum_b.shape, bf16), vm(sum_l.shape, f32),
+                *[vm(s, f32) for s in results], dma((4 + count * parts,)), dma((4 + count * parts,))],
             compiler_params=pltpu.CompilerParams(vmem_limit_bytes=60 * 2**20),
         )(timesteps, grad, sum_a, sum_b, sum_l)
 

time: 66.1 us -> 62.3 us (0.943); the launches traced: 65.9 us -> 61.2 us
  Pallas kernels: 65 us -> 60.4 us
    pallas_call x1, Pallas kernels: 60.5 us -> 56.5 us  [body(): pl.pallas_call(functools.partial(kernel, (nr, nc)), out_shape=[shape(late...]
where the time goes in v3:
time: 62.3 us; the launch traced here: 61.2 us
  Pallas kernels  60.4 us (97%)
  between operations  0.8 us (1%)
    pallas_call x1, Pallas kernels, body(): pl.pallas_call(functools.partial(kernel, (nr, nc)), out_shape=[shape(late...  56.5 us
    pallas_call x1, Pallas kernels, body(): pl.pallas_call(functools.partial(finishing, factor, parts), out_shape=[sh...  3.92 us

profile of v3, /device:TPU:1, one launch (start us, length us, event | category | flops | bytes accessed | tf_op | source)
XLA Modules:
  0.0 61.2 jit_solution(16771751008984311471)
XLA Ops:
  0.6 56.5 %shard_map.110 = (bf16[2,64,64,128]{3,2,1,0:T(8,128)(2,1)}, bf16[10,128,256]{2,1,0:T(8,128)(2,1)}, bf16[10,128,128]{2,1,0:T(8,128)(2,1)}, f32[8,128]{1,0:T(8,128)}) custom-call(s32[2]{0:T(128)} %times_in.3, bf16[2,64,64,128]{3,2,1,0:T(8,128)(2,1)} %lat_in.1, bf16[2,64,64,128]{3,2,1,0:T(8,128)(2,1)} %cot_in.1, f32[1000,128]{1,0:T(8,128)} %table_in.1, ...), custom_call_target="tpu_custom_call" | custom-call | tf_op jit(solution)/shard_map/pallas_call | solution.py:650
  57.1 3.9 %shard_map.111 = (f32[2,64,64,128]{3,2,1,0:T(8,128)}, f32[3,3,128,128]{3,2,1,0:T(8,128)}, f32[3,3,128,256]{3,2,1,0:T(8,128)}, f32[256,128]{1,0:T(8,128)}, f32[1000,128]{1,0:T(8,128)}) custom-call(s32[2]{0:T(128)} %times_in.3, bf16[2,64,64,128]{3,2,1,0:T(8,128)(2,1)} %get-tuple-element.9.grad_in, bf16[10,128,256]{2,1,0:T(8,128)(2,1)} %get-tuple-element.10.a_in, ...), custom_call_target="tpu_custom_call" | custom-call | tf_op jit(solution)/shard_map/pallas_call | solution.py:663

commit v4 on v3

--- a/solution.py
+++ b/solution.py
@@ -39,7 +39,7 @@
     times, lat, cot, table, kfine, kcoarse, lift,
     w_fwd, w_back, wc_back, lift_hi, lift_lo,
     V, C2, SL, PO, UG, CB, ACT, GC, G, OUT,
-    sc_v, rc_v, sc_p, rc_p, sc_c, rc_c, sc_g, rc_g,
+    sc_v, rc_v, sc_p, rc_p, sc_c, rc_c, sc_g, rc_g, er_p, er_c,
     a_theirs, a_mixed, a_send, a_r1, a_s2, a_r2, a_t, a_f,
     b_send, b_r1, b_s2, b_r2, b_t, b_f,
     l_send, l_r1, l_s2, l_r2, l_f,
@@ -82,11 +82,14 @@
         return pltpu.make_async_remote_copy(
             src_ref=src, dst_ref=dst, send_sem=ssem, recv_sem=rsem, device_id=who, device_id_type=MESH)
 
-    def exchange(kind, b, buf, n, lo, hi, sc, rc):
+    def exchange(kind, b, buf, n, lo, hi, sc, rc, edges=None):
         at = kind * count + b
         first_col, last_col = sc.at[b, 0], sc.at[b, 1]
         to_left, to_right = rc.at[b, 1], rc.at[b, 0]
         lanes = pl.ds(lo, hi - lo)
+        first_row, last_row = buf.at[b, 1, :, lanes], buf.at[b, n, :, lanes]
+        if edges is not None:
+            first_row, last_row = edges.at[b, 0], edges.at[b, 1]
         plan = [
             (first_col.at[pl.ds(0, 8)], to_left.at[pl.ds(n + 8, 8)], (up, left)),
             (last_col.at[pl.ds(0, 8)], to_right.at[pl.ds(n + 8, 8)], (up, right)),
@@ -94,8 +97,8 @@
             (last_col.at[pl.ds(n - 8, 8)], to_right.at[pl.ds(0, 8)], (down, right)),
             (first_col, to_left.at[pl.ds(8, n)], (row, left)),
             (last_col, to_right.at[pl.ds(8, n)], (row, right)),
-            (buf.at[b, 1, :, lanes], buf.at[b, n + 1, :, lanes], (up, col)),
-            (buf.at[b, n, :, lanes], buf.at[b, 0, :, lanes], (down, col)),
+            (first_row, buf.at[b, n + 1, :, lanes], (up, col)),
+            (last_row, buf.at[b, 0, :, lanes], (down, col)),
         ]
         rows = sum(math.prod(src.shape) * jnp.dtype(src.dtype).itemsize for src, _, _ in plan) // (4 * chans)
         every = table.at[pl.ds(0, rows)]
@@ -146,12 +149,6 @@
     def columns_fine(buf, b, sc):
         sc[b, 0] = buf[b, 1 : tall + 1, 0:16, chans : 2 * chans].astype(f32)[:, 0, :]
         sc[b, 1] = buf[b, 1 : tall + 1, half - 16 : half, 2 * chans : 3 * chans].astype(f32)[:, 15, :]
-
-    def columns_coarse(buf, b, sc):
-        wide_by = sc.shape[3]
-        lanes = slice(wide_by, 2 * wide_by)
-        sc[b, 0] = buf[b, 1 : low + 1, 0:16, lanes].astype(f32)[:, 0, :]
-        sc[b, 1] = buf[b, 1 : low + 1, half - 16 : half, lanes].astype(f32)[:, 15, :]
 
     def split_latents(b):
         V[b, 1 : tall + 1, :, chans : 3 * chans] = lat[b].reshape(tall, half, 2 * chans)
@@ -218,6 +215,41 @@
             return 0
 
         lax.fori_loop(0, tall // step, one, 0)
+
+    def border_columns(buf, b, n):
+        strips = []
+        for at in (0, 15):
+            lo = at // 15 * (half - 16)
+            strip = buf[b, :, lo : lo + 16, :].astype(f32)[:, at, :]
+            strips.append(jnp.concatenate([strip[i : i + n] for i in range(3)], -1).astype(bf16))
+        return strips
+
+    def border_rows(buf, b, first, rows):
+        taps = [buf[b, first + i : first + i + rows].reshape(rows * half, buf.shape[3]) for i in range(3)]
+        return jnp.concatenate(taps, -1)
+
+    def fine_border(b):
+        embedding = table[pl.ds(times[b], 1), :]
+        embedding = jnp.concatenate([embedding, embedding], -1)
+        taps = border_columns(V, b, tall) + [border_rows(V, b, 0, 2), border_rows(V, b, tall - 2, 2)]
+        pre = dot(jnp.concatenate(taps, 0), w_fwd[...]) + embedding
+        hidden = (pre * sigmoid(pre)).astype(bf16).astype(f32)
+        across = hidden[: 2 * tall].reshape(2 * low, 2, 2 * chans).sum(axis=1)
+        across = (0.25 * (across[:, :chans] + across[:, chans:])).astype(bf16).astype(f32)
+        sc_p[b, 0], sc_p[b, 1] = across[:low], across[low:]
+        along = hidden[2 * tall :].reshape(2, 2, half, 2 * chans).sum(axis=1)
+        er_p[b] = (0.25 * (along[:, :, :chans] + along[:, :, chans:])).astype(bf16)
+
+    def coarse_border(b):
+        taps = border_columns(PO, b, low) + [border_rows(PO, b, 0, 1), border_rows(PO, b, low - 1, 1)]
+        pre = dot(jnp.concatenate(taps, 0), kcoarse[...].reshape(9 * chans, 2 * chans))
+        s = sigmoid(pre)
+        back = CB[b].reshape(low, half, 2 * chans)
+        back = [back[:, 0, :], back[:, half - 1, :], back[0], back[low - 1]]
+        grad = jnp.concatenate(back, 0) * (s + pre * s * (1.0 - s))
+        grad = grad.astype(bf16)
+        sc_c[b, 0], sc_c[b, 1] = grad[:low].astype(f32), grad[low : 2 * low].astype(f32)
+        er_c[b, 0], er_c[b, 1] = grad[2 * low : 2 * low + half], grad[2 * low + half :]
 
     def forward_coarse(b):
         step = 32
@@ -425,31 +457,32 @@
     split_cotangent(0)
     loads["cot1"].wait()
     split_cotangent(1)
-    loads["table"].wait()
-    loads["times"].wait()
-    loads["kcoarse"].wait()
-
-    moving_p = [exchange(1, *ex_p[b], sc_p, rc_p) for b in range(count)]
-    for b in range(count):
-        arrive(moving_v[b], *ex_v[b], rc_v)
-        widen_fine(V, b, rc_v)
-        forward_fine(b)
-        columns_coarse(PO, b, sc_p)
-        send(moving_p[b])
-
     loads["lift"].wait()
     prepare_lift()
     lift_back(0)
     lift_back(1)
+    loads["kcoarse"].wait()
     prepare_back()
-
-    moving_c = [exchange(2, *ex_c[b], sc_c, rc_c) for b in range(count)]
+    loads["table"].wait()
+    loads["times"].wait()
+
+    moving_p = [exchange(1, *ex_p[b], sc_p, rc_p, er_p) for b in range(count)]
+    for b in range(count):
+        arrive(moving_v[b], *ex_v[b], rc_v)
+        widen_fine(V, b, rc_v)
+        fine_border(b)
+        send(moving_p[b])
+    for b in range(count):
+        forward_fine(b)
+
+    moving_c = [exchange(2, *ex_c[b], sc_c, rc_c, er_c) for b in range(count)]
     for b in range(count):
         arrive(moving_p[b], *ex_p[b], rc_p)
         widen_coarse(PO, b, rc_p)
+        coarse_border(b)
+        send(moving_c[b])
+    for b in range(count):
         forward_coarse(b)
-        columns_coarse(GC, b, sc_c)
-        send(moving_c[b])
 
     lifted = jnp.zeros((2 * chans, 2 * chans), f32)
     for b in range(count):
@@ -639,6 +672,7 @@
             vm((count, tall + 2, half, 4 * chans), bf16),
             vm(latents.shape, bf16),
             *columns(tall, chans), *columns(low, chans), *columns(low, 2 * chans), *columns(tall, chans),
+            vm((count, 2, half, chans), bf16), vm((count, 2, half, 2 * chans), bf16),
             vm((5, chans, 2 * chans), f32), vm((5, chans, 2 * chans), bf16),
             *reducer(2 * chans, nr, f32), *reducer(chans, 2 * nr, bf16),
             vm((8, chans), f32), vm((2 * nr, 8, chans), f32), vm((8, chans), f32), vm((pairs, 8, chans), f32),

time: 62.3 us -> 61.3 us (0.984); the launches traced: 61.2 us -> 61.1 us
  no operation moved by 1% of the time
where the time goes in v4:
time: 61.3 us; the launch traced here: 61.1 us
  Pallas kernels  60.3 us (98%)
  between operations  0.8 us (1%)
    pallas_call x1, Pallas kernels, body(): pl.pallas_call(functools.partial(kernel, (nr, nc)), out_shape=[shape(late...  56.4 us
    pallas_call x1, Pallas kernels, body(): pl.pallas_call(functools.partial(finishing, factor, parts), out_shape=[sh...  3.92 us

profile of v4, /device:TPU:1, one launch (start us, length us, event | category | flops | bytes accessed | tf_op | source)
XLA Modules:
  0.0 61.1 jit_solution(16598001152304211458)
XLA Ops:
  0.6 56.4 %shard_map.110 = (bf16[2,64,64,128]{3,2,1,0:T(8,128)(2,1)}, bf16[10,128,256]{2,1,0:T(8,128)(2,1)}, bf16[10,128,128]{2,1,0:T(8,128)(2,1)}, f32[8,128]{1,0:T(8,128)}) custom-call(s32[2]{0:T(128)} %times_in.3, bf16[2,64,64,128]{3,2,1,0:T(8,128)(2,1)} %lat_in.1, bf16[2,64,64,128]{3,2,1,0:T(8,128)(2,1)} %cot_in.1, f32[1000,128]{1,0:T(8,128)} %table_in.1, ...), custom_call_target="tpu_custom_call" | custom-call | tf_op jit(solution)/shard_map/pallas_call | solution.py:684
  57.0 3.9 %shard_map.111 = (f32[2,64,64,128]{3,2,1,0:T(8,128)}, f32[3,3,128,128]{3,2,1,0:T(8,128)}, f32[3,3,128,256]{3,2,1,0:T(8,128)}, f32[256,128]{1,0:T(8,128)}, f32[1000,128]{1,0:T(8,128)}) custom-call(s32[2]{0:T(128)} %times_in.3, bf16[2,64,64,128]{3,2,1,0:T(8,128)(2,1)} %get-tuple-element.9.grad_in, bf16[10,128,256]{2,1,0:T(8,128)(2,1)} %get-tuple-element.10.a_in, ...), custom_call_target="tpu_custom_call" | custom-call | tf_op jit(solution)/shard_map/pallas_call | solution.py:697

commit v5 on v4

--- a/solution.py
+++ b/solution.py
@@ -201,7 +201,7 @@
     def forward_fine(b):
         embedding = table[pl.ds(times[b], 1), :]
         embedding = jnp.concatenate([embedding, embedding], -1)
-        step = 32
+        step = 64
 
         def one(k, _):
             taps = [V[b, pl.ds(k * step + i, step)].reshape(step * half, 4 * chans) for i in range(3)]
@@ -510,17 +510,6 @@
         if b == 0:
             sum_a.scatter_rows()
 
-    l_send[...] = jnp.concatenate(sums + [jnp.zeros((8 - count, chans), f32)], 0)
-    l_moving = [
-        remote(l_send, l_r1.at[2 * row + core], l_ssem.at[0], l_rsem.at[0],
-               (lax.rem(row + at // 2, nr), twin if at % 2 else col))
-        for at in range(1, 2 * nr)
-    ]
-    every = l_r1.at[pl.ds(0, 2 * nr - 1)]
-    l_moving = l_moving, remote(every, every, l_ssem.at[0], l_rsem.at[0], (row, twin))
-    send(l_moving)
-    l_r1[2 * row + core] = l_send[...]
-
     for i in range(3):
         kernel_grad = jnp.zeros((2 * chans, 4 * chans), f32)
         for b in range(count):
@@ -535,11 +524,23 @@
     b_send[9] = jnp.zeros(b_send.shape[1:], bf16)
     sum_b.scatter(1)
 
+    l_send[...] = jnp.concatenate(sums + [jnp.zeros((8 - count, chans), f32)], 0)
+    l_moving = [
+        remote(l_send, l_r1.at[2 * row + core], l_ssem.at[0], l_rsem.at[0],
+               (lax.rem(row + at // 2, nr), twin if at % 2 else col))
+        for at in range(1, 2 * nr)
+    ]
+    every = l_r1.at[pl.ds(0, 2 * nr - 1)]
+    l_moving = l_moving, remote(every, every, l_ssem.at[0], l_rsem.at[0], (row, twin))
+    send(l_moving)
+    l_r1[2 * row + core] = l_send[...]
+
     arrive(moving_g[0], *ex_g[0], rc_g)
     widen_fine(G, 0, rc_g)
-    sum_a.cross()
     backward_fine(0, 0, 2)
     backward_fine(0, 1, 2)
+    sum_a.cross()
+    sum_b.cross()
     l_moving[1].wait_recv()
     total = l_r1[0]
     for at in range(1, 2 * nr):
@@ -558,7 +559,6 @@
     arrive(moving_g[1], *ex_g[1], rc_g)
     widen_fine(G, 1, rc_g)
     backward_fine(1, 0, 2)
-    sum_b.cross()
     backward_fine(1, 1, 2)
     sum_a.gather()
     sum_b.gather()

time: 61.3 us -> 60.9 us (level)
  no operation moved by 1% of the time
where the time goes in v5:
time: 60.9 us; the launch traced here: 60.8 us
  Pallas kernels  60 us (99%)
  between operations  0.8 us (1%)
    pallas_call x1, Pallas kernels, body(): pl.pallas_call(functools.partial(kernel, (nr, nc)), out_shape=[shape(late...  56 us
    pallas_call x1, Pallas kernels, body(): pl.pallas_call(functools.partial(finishing, factor, parts), out_shape=[sh...  3.92 us

profile of v5, /device:TPU:1, one launch (start us, length us, event | category | flops | bytes accessed | tf_op | source)
XLA Modules:
  0.0 60.8 jit_solution(6088409382160944911)
XLA Ops:
  0.6 56.0 %shard_map.110 = (bf16[2,64,64,128]{3,2,1,0:T(8,128)(2,1)}, bf16[10,128,256]{2,1,0:T(8,128)(2,1)}, bf16[10,128,128]{2,1,0:T(8,128)(2,1)}, f32[8,128]{1,0:T(8,128)}) custom-call(s32[2]{0:T(128)} %times_in.3, bf16[2,64,64,128]{3,2,1,0:T(8,128)(2,1)} %lat_in.1, bf16[2,64,64,128]{3,2,1,0:T(8,128)(2,1)} %cot_in.1, f32[1000,128]{1,0:T(8,128)} %table_in.1, ...), custom_call_target="tpu_custom_call" | custom-call | tf_op jit(solution)/shard_map/pallas_call | solution.py:684
  56.7 3.9 %shard_map.111 = (f32[2,64,64,128]{3,2,1,0:T(8,128)}, f32[3,3,128,128]{3,2,1,0:T(8,128)}, f32[3,3,128,256]{3,2,1,0:T(8,128)}, f32[256,128]{1,0:T(8,128)}, f32[1000,128]{1,0:T(8,128)}) custom-call(s32[2]{0:T(128)} %times_in.3, bf16[2,64,64,128]{3,2,1,0:T(8,128)(2,1)} %get-tuple-element.9.grad_in, bf16[10,128,256]{2,1,0:T(8,128)(2,1)} %get-tuple-element.10.a_in, ...), custom_call_target="tpu_custom_call" | custom-call | tf_op jit(solution)/shard_map/pallas_call | solution.py:697

commit v6 on v4

--- a/solution.py
+++ b/solution.py
@@ -39,7 +39,7 @@
     times, lat, cot, table, kfine, kcoarse, lift,
     w_fwd, w_back, wc_back, lift_hi, lift_lo,
     V, C2, SL, PO, UG, CB, ACT, GC, G, OUT,
-    sc_v, rc_v, sc_p, rc_p, sc_c, rc_c, sc_g, rc_g, er_p, er_c,
+    sc_v, rc_v, sc_p, rc_p, sc_c, rc_c, sc_g, rc_g, er_p,
     a_theirs, a_mixed, a_send, a_r1, a_s2, a_r2, a_t, a_f,
     b_send, b_r1, b_s2, b_r2, b_t, b_f,
     l_send, l_r1, l_s2, l_r2, l_f,
@@ -239,17 +239,6 @@
         sc_p[b, 0], sc_p[b, 1] = across[:low], across[low:]
         along = hidden[2 * tall :].reshape(2, 2, half, 2 * chans).sum(axis=1)
         er_p[b] = (0.25 * (along[:, :, :chans] + along[:, :, chans:])).astype(bf16)
-
-    def coarse_border(b):
-        taps = border_columns(PO, b, low) + [border_rows(PO, b, 0, 1), border_rows(PO, b, low - 1, 1)]
-        pre = dot(jnp.concatenate(taps, 0), kcoarse[...].reshape(9 * chans, 2 * chans))
-        s = sigmoid(pre)
-        back = CB[b].reshape(low, half, 2 * chans)
-        back = [back[:, 0, :], back[:, half - 1, :], back[0], back[low - 1]]
-        grad = jnp.concatenate(back, 0) * (s + pre * s * (1.0 - s))
-        grad = grad.astype(bf16)
-        sc_c[b, 0], sc_c[b, 1] = grad[:low].astype(f32), grad[low : 2 * low].astype(f32)
-        er_c[b, 0], er_c[b, 1] = grad[2 * low : 2 * low + half], grad[2 * low + half :]
 
     def forward_coarse(b):
         step = 32
@@ -475,14 +464,15 @@
     for b in range(count):
         forward_fine(b)
 
-    moving_c = [exchange(2, *ex_c[b], sc_c, rc_c, er_c) for b in range(count)]
+    moving_c = [exchange(2, *ex_c[b], sc_c, rc_c) for b in range(count)]
     for b in range(count):
         arrive(moving_p[b], *ex_p[b], rc_p)
         widen_coarse(PO, b, rc_p)
-        coarse_border(b)
+        forward_coarse(b)
+        here = slice(2 * chans, 4 * chans)
+        sc_c[b, 0] = GC[b, 1 : low + 1, 0:16, here].astype(f32)[:, 0, :]
+        sc_c[b, 1] = GC[b, 1 : low + 1, half - 16 : half, here].astype(f32)[:, 15, :]
         send(moving_c[b])
-    for b in range(count):
-        forward_coarse(b)
 
     lifted = jnp.zeros((2 * chans, 2 * chans), f32)
     for b in range(count):
@@ -672,7 +662,7 @@
             vm((count, tall + 2, half, 4 * chans), bf16),
             vm(latents.shape, bf16),
             *columns(tall, chans), *columns(low, chans), *columns(low, 2 * chans), *columns(tall, chans),
-            vm((count, 2, half, chans), bf16), vm((count, 2, half, 2 * chans), bf16),
+            vm((count, 2, half, chans), bf16),
             vm((5, chans, 2 * chans), f32), vm((5, chans, 2 * chans), bf16),
             *reducer(2 * chans, nr, f32), *reducer(chans, 2 * nr, bf16),
             vm((8, chans), f32), vm((2 * nr, 8, chans), f32), vm((8, chans), f32), vm((pairs, 8, chans), f32),

time: 61.3 us -> 62.2 us (1.015)
  Pallas kernels: 60.3 us -> 61.2 us
    pallas_call x1, Pallas kernels: 56.4 us -> 57.3 us  [body(): pl.pallas_call(functools.partial(kernel, (nr, nc)), out_shape=[shape(late...]
where the time goes in v6:
time: 62.2 us; the launch traced here: 62 us
  Pallas kernels  61.2 us (98%)
  between operations  0.8 us (1%)
    pallas_call x1, Pallas kernels, body(): pl.pallas_call(functools.partial(kernel, (nr, nc)), out_shape=[shape(late...  57.3 us
    pallas_call x1, Pallas kernels, body(): pl.pallas_call(functools.partial(finishing, factor, parts), out_shape=[sh...  3.92 us

profile of v6, /device:TPU:1, one launch (start us, length us, event | category | flops | bytes accessed | tf_op | source)
XLA Modules:
  0.0 62.0 jit_solution(4756646108828151233)
XLA Ops:
  0.6 57.3 %shard_map.110 = (bf16[2,64,64,128]{3,2,1,0:T(8,128)(2,1)}, bf16[10,128,256]{2,1,0:T(8,128)(2,1)}, bf16[10,128,128]{2,1,0:T(8,128)(2,1)}, f32[8,128]{1,0:T(8,128)}) custom-call(s32[2]{0:T(128)} %times_in.3, bf16[2,64,64,128]{3,2,1,0:T(8,128)(2,1)} %lat_in.1, bf16[2,64,64,128]{3,2,1,0:T(8,128)(2,1)} %cot_in.1, f32[1000,128]{1,0:T(8,128)} %table_in.1, ...), custom_call_target="tpu_custom_call" | custom-call | tf_op jit(solution)/shard_map/pallas_call | solution.py:674
  57.9 3.9 %shard_map.111 = (f32[2,64,64,128]{3,2,1,0:T(8,128)}, f32[3,3,128,128]{3,2,1,0:T(8,128)}, f32[3,3,128,256]{3,2,1,0:T(8,128)}, f32[256,128]{1,0:T(8,128)}, f32[1000,128]{1,0:T(8,128)}) custom-call(s32[2]{0:T(128)} %times_in.3, bf16[2,64,64,128]{3,2,1,0:T(8,128)(2,1)} %get-tuple-element.9.grad_in, bf16[10,128,256]{2,1,0:T(8,128)(2,1)} %get-tuple-element.10.a_in, ...), custom_call_target="tpu_custom_call" | custom-call | tf_op jit(solution)/shard_map/pallas_call | solution.py:687
